TPU v7x, 768 devices: a whole 4x8x12 slice. The times are simulated.
768 devices in a mesh: grp: 8 (over y), dev: 96 (over x, z, core).
Axes of the slice: x: 4, y: 8, z: 12, core: 2. Of those that a mesh axis runs over, the one named last changes fastest.
Arguments:
- sensitivity: float32 [768, 16, 128, 128], P(('grp', 'dev')), may hold values from -0.2 to 0.2
- tile_rows: int32 [768, 16], P(('grp', 'dev')), may hold values from 0 to 15
- tile_cols: int32 [768, 16], P(('grp', 'dev')), may hold values from 0 to 1535, as said below
- tile_count: int32 [768], P(('grp', 'dev')), may hold values from 1 to 16, as said below
- travel_times: float32 [12288, 128], P(('grp', 'dev')), may hold values from -6 to 6
Outputs:
- model_update: float32 [1536, 128], P(('grp', 'dev'))
- residual_ratio: float32 [1], replicated
Inputs may be any that keep to these rules, and one draw needn't show every extreme that they name: `tile_cols`: A tile stored on a device of region g (its grp index) names a column block of the slabs of regions g - 1, g or g + 1, the slab of region h being blocks h * 192 to (h + 1) * 192 - 1. `tile_count`: some device has all 16 slots live.
All inputs are finite; a program needn't handle non-finite values.
Results may differ from a plain program's by a relative error of at most 0.0035.
Values sent between devices are 32-bit elements; how exact they have to be, the bound alone decides.
No kernel may reach another device: no remote copies, remote signals or barrier semaphores. Data moves between devices by JAX's collectives and lax.ppermute only.
A program may use at most 32 MiB of HBM per device.

v0:
```python
import jax
import jax.numpy as jnp
from jax import lax
from jax.sharding import PartitionSpec as P

CB_DEV = 2
ITERS = 2


def extended(cells, sides, width):
    for axis, dim in sides:
        count = lax.axis_size(axis)
        ends = count - 1
        head = lax.slice_in_dim(cells, 0, width, axis=dim)
        tail = lax.slice_in_dim(cells, cells.shape[dim] - width, cells.shape[dim], axis=dim)
        cells = jnp.concatenate(
            [
                lax.ppermute(tail, axis, [(i, (i + 1) % count) for i in range(ends)]),
                cells,
                lax.ppermute(head, axis, [((i + 1) % count, i) for i in range(ends)]),
            ],
            axis=dim,
        )
    return cells


def local(sensitivity, tile_rows, tile_cols, tile_count, travel_times):
    tile_set = sensitivity[0]
    row_ids = tile_rows[0]
    column_ids = tile_cols[0]
    live_count = tile_count[0]
    slot_total = tile_set.shape[0]
    row_blocks = travel_times.shape[0]
    dev_size = lax.axis_size("dev")
    is_live = jnp.arange(slot_total, dtype=jnp.int32) < live_count
    row_onehot = (row_ids[None, :] == jnp.arange(row_blocks, dtype=jnp.int32)[:, None]).astype(
        jnp.float32
    )

    def forward(cell_table, cell_index):
        picked = jnp.take(cell_table, cell_index, axis=0)
        product = jnp.einsum("kij,kj->ki", tile_set, picked, precision=lax.Precision.HIGHEST)
        product = jnp.where(is_live[:, None], product, jnp.float32(0.0))
        return jnp.dot(row_onehot, product, precision=lax.Precision.HIGHEST)

    def tile_terms(ray_vec):
        picked = jnp.take(ray_vec, row_ids, axis=0)
        product = jnp.einsum("kij,ki->kj", tile_set, picked, precision=lax.Precision.HIGHEST)
        return jnp.where(is_live[:, None], product, jnp.float32(0.0))

    def backward(ray_vec, cell_index, cell_total):
        return jax.ops.segment_sum(tile_terms(ray_vec), cell_index, num_segments=cell_total)

    region = lax.axis_index("grp")
    slab_size = CB_DEV * dev_size
    column_region = column_ids // slab_size
    within = column_ids % slab_size
    local_index = (
        within // CB_DEV * (3 * CB_DEV) + (column_region - region + 1) * CB_DEV + within % CB_DEV
    )

    def transpose(ray_vec):
        partial_value = backward(ray_vec, local_index, dev_size * 3 * CB_DEV)
        own_share = lax.psum_scatter(partial_value, "dev", scatter_dimension=0, tiled=True)
        rim_terms = extended(own_share, (("grp", 0),), CB_DEV)
        return rim_terms[:CB_DEV] + rim_terms[2 * CB_DEV : 3 * CB_DEV] + rim_terms[4 * CB_DEV :]

    def advance(raw_cells, ray_vec):
        rim_cells = extended(raw_cells, (("grp", 0),), CB_DEV)
        cell_table = lax.all_gather(rim_cells, "dev", axis=0, tiled=True)
        image = forward(cell_table, local_index)
        sum_cells, sum_image, sum_cross = lax.psum(
            (jnp.sum(raw_cells * raw_cells), jnp.sum(image * image), jnp.sum(image * ray_vec)),
            ("grp", "dev"),
        )
        alpha_now = jnp.sqrt(sum_cells)
        beta_now = jnp.sqrt(sum_image / sum_cells - 2.0 * sum_cross + sum_cells)
        residue = image / alpha_now - alpha_now * ray_vec
        return (alpha_now, beta_now, residue)

    beta_first = jnp.sqrt(lax.psum(jnp.sum(travel_times * travel_times), ("grp", "dev")))
    ray_vec = travel_times / beta_first
    raw_cells = transpose(ray_vec)
    alpha_now, beta_now, residue = advance(raw_cells, ray_vec)
    cell_vec = raw_cells / alpha_now
    direction = cell_vec
    solution = jnp.zeros_like(cell_vec)
    phi_bar = beta_first
    rho_bar = alpha_now
    for iteration in range(ITERS):
        ray_vec = residue / beta_now
        if iteration + 1 < ITERS:
            raw_cells = transpose(ray_vec) - beta_now * cell_vec
            alpha_next, beta_next, residue = advance(raw_cells, ray_vec)
            cell_next = raw_cells / alpha_next
        rho_val = jnp.sqrt(rho_bar * rho_bar + beta_now * beta_now)
        cosine = rho_bar / rho_val
        sine_val = beta_now / rho_val
        phi_val = cosine * phi_bar
        phi_bar = sine_val * phi_bar
        solution = solution + phi_val / rho_val * direction
        if iteration + 1 < ITERS:
            rho_bar = -cosine * alpha_next
            direction = cell_next - sine_val * alpha_next / rho_val * direction
            cell_vec = cell_next
            beta_now = beta_next
    return (solution, (phi_bar / beta_first).reshape(1))


def solution(mesh):
    in_specs = (
        P(("grp", "dev"), None, None, None),
        P(("grp", "dev"), None),
        P(("grp", "dev"), None),
        P(("grp", "dev")),
        P(("grp", "dev"), None),
    )
    out_specs = (P(("grp", "dev"), None), P())
    return jax.shard_map(local, mesh=mesh, in_specs=in_specs, out_specs=out_specs, check_vma=False)
```

profile of v0, /device:TPU:1, one launch (start us, length us, event | category | flops | bytes accessed | tf_op | source)
XLA Modules:
  0.0 1044.2 jit_solution(9823848947049428569)
XLA Ops:
  8.0 1.4 multiply_reduce_fusion.4
  9.3 120.5 %psum.49 = f32[]{:T(128)} all-reduce(f32[]{:T(128)} %multiply_reduce_fusion.4), channel_id=1, replica_groups=mesh['grp'=8,'dev'=96] {'grp','dev'}, use_global_device_ids=true, to_apply=%region_1.2 | all-reduce | flops 1 | bytes 8 | tf_op jit(solution)/shard_map/psum | solution.py:81
  132.8 1.4 scatter_custom_fusion
  136.2 249.7 %all-reduce.7.cloned.1.call-done = f32[576,128]{1,0:T(8,128)} async-done(((f32[576,128]{1,0:T(8,128)}), f32[576,128]{1,0:T(8,128)}) %all-reduce.7.cloned.1.call-update) | async-done | bytes 294928
  386.7 3.1 collective-permute-start
  389.8 1.3 collective-permute-start.1
  391.1 3.0 collective-permute-done.1
  394.7 3.1 collective-permute-start.2
  397.8 1.3 collective-permute-start.3
  399.1 3.7 collective-permute-done.3
  402.8 65.5 %all-gather = f32[96,6,128]{2,1,0:T(8,128)S(1)} all-gather(f32[1,6,128]{2,1,0:T(8,128)S(1)} %maximum_bitcast_fusion), channel_id=1, replica_groups=mesh['grp'=8,'dev'=96] {'dev'}, dimensions={0}, use_global_device_ids=true | all-gather | bytes 297984 | tf_op jit(solution)/shard_map/all_gather | solution.py:70
  469.0 1.7 fusion.4
  471.7 104.6 %all-reduce.3 = (f32[]{:T(128)}, f32[]{:T(128)}, f32[]{:T(128)}) all-reduce(f32[]{:T(128)} %get-tuple-element.7, f32[]{:T(128)} %get-tuple-element.16, f32[]{:T(128)} %get-tuple-element.6), channel_id=1, replica_groups=mesh['grp'=8,'dev'=96] {'grp','dev'}, use_global_device_ids=true, to_apply=%region_7.10 | all-reduce | flops 3 | bytes 24 | tf_op jit(solution)/shard_map/psum | solution.py:72
  581.2 1.4 scatter_custom_fusion.1
  582.6 259.2 %all-reduce.9.cloned.1.call-done = f32[576,128]{1,0:T(8,128)} async-done(((f32[576,128]{1,0:T(8,128)}), f32[576,128]{1,0:T(8,128)}) %all-reduce.9.cloned.1.call-update) | async-done | bytes 294928
  842.5 3.1 collective-permute-start.4
  845.7 1.3 collective-permute-start.5
  847.0 3.0 collective-permute-done.5
  850.6 3.1 collective-permute-start.6
  853.7 1.3 collective-permute-start.7
  855.2 3.5 collective-permute-done.7
  858.7 65.5 %all-gather.1 = f32[96,6,128]{2,1,0:T(8,128)S(1)} all-gather(f32[1,6,128]{2,1,0:T(8,128)S(1)} %maximum_bitcast_fusion.1), channel_id=1, replica_groups=mesh['grp'=8,'dev'=96] {'dev'}, dimensions={0}, use_global_device_ids=true | all-gather | bytes 297984 | tf_op jit(solution)/shard_map/all_gather | solution.py:70
  924.9 1.7 fusion
  927.6 104.6 %all-reduce.2 = (f32[]{:T(128)}, f32[]{:T(128)}, f32[]{:T(128)}) all-reduce(f32[]{:T(128)} %get-tuple-element.14, f32[]{:T(128)} %get-tuple-element.5, f32[]{:T(128)} %get-tuple-element.4), channel_id=1, replica_groups=mesh['grp'=8,'dev'=96] {'grp','dev'}, use_global_device_ids=true, to_apply=%region_13.16 | all-reduce | flops 3 | bytes 24 | tf_op jit(solution)/shard_map/psum | solution.py:72
  (49 shorter events, 11.8 us)
Async XLA Ops:
  7.2 124.7 %copy-start = (f32[1,16,128,128]{3,2,1,0:T(8,128)S(1)}, f32[1,16,128,128]{3,2,1,0:T(8,128)}, u32[]{:S(2)}) copy-start(f32[1,16,128,128]{3,2,1,0:T(8,128)} %param.9) | copy-start | bytes 3145732
  7.2 0.8 copy-start.3
  7.2 378.8 %all-reduce.7.cloned.1.call-start = ((), (), s32[]{:S(2)}) async-start(), calls=%async_computation | async-start | bytes 589824
  8.0 122.5 %copy-start.1 = (f32[16,128]{1,0:T(8,128)S(1)}, f32[16,128]{1,0:T(8,128)}, u32[]{:S(2)}) copy-start(f32[16,128]{1,0:T(8,128)} %param.13) | copy-start | bytes 24580
  131.8 1.0 copy-start.2
  134.3 707.6 %all-reduce.9.cloned.1.call-start = ((), (), s32[]{:S(2)}) async-start(), calls=%async_computation.1 | async-start | bytes 589824
  386.7 4.4 collective-permute-start
  389.8 4.3 collective-permute-start.1
  394.7 4.4 collective-permute-start.2
  397.8 5.0 collective-permute-start.3
  842.5 4.4 collective-permute-start.4
  845.7 4.3 collective-permute-start.5
  850.6 4.6 collective-permute-start.6
  853.7 5.0 collective-permute-start.7
Sparse Core Ops, SparseCore 0:
  134.4 251.5 all-reduce.6
  582.7 259.0 all-reduce.8
where the time goes:
time: 1050 us; the launch traced here: 1040 us
  waiting for transfers between devices  522 us (50%)
  blocking collectives  461 us (44%)
  between operations  24.4 us (2%)
  starting transfers between devices  17.6 us (2%)
    unnamed x4, waiting for transfers between devices  509 us
    psum x2, blocking collectives, advance(): lax.psum((jnp.sum(raw_cells * raw_cells), jnp.sum(image * image), jnp.sum...  209 us
    all_gather x2, blocking collectives, advance(): cell_table = lax.all_gather(rim_cells, 'dev', axis=0, tiled=True)  131 us
    psum x1, blocking collectives, local(): lax.psum(jnp.sum(travel_times * travel_times), ('grp', 'dev'))  120 us
  transfers between devices with their start and end apart: 10, of which 6 were waited for; matrix products, arithmetic and copies ran while one was open for 0% of the time, Pallas kernels for 0%

commit v1 on v0

v1 whole, which is shorter than its diff:
```python
import jax
import jax.numpy as jnp
from jax import lax
from jax.sharding import Mesh, PartitionSpec as P

NY, NX, NZ, NC = 8, 4, 12, 2
SLAB = 192
JB = SLAB // (NC * NZ)
SLOT = 3 * JB
LANES = 128
TABLE = NC * NZ * SLOT


def reduce_table(table, scalars, y):
    core = lax.axis_index("c")
    table = table.reshape(NC, NZ, SLOT, LANES)
    row = jnp.zeros((JB, LANES), jnp.float32)
    for i, value in enumerate(scalars):
        row = row.at[0, i].set(value)
    table = jnp.concatenate([table, jnp.broadcast_to(row, (NC, NZ, JB, LANES))], axis=2)
    pair = lax.all_gather(table, "c", axis=0, tiled=False)
    half = lax.dynamic_index_in_dim(pair, core, axis=1, keepdims=False).sum(0)
    part = lax.all_to_all(half, "z", 0, 0, tiled=True).sum(0)
    wide = lax.all_to_all(
        jnp.broadcast_to(part[None], (NY * NX, SLOT + JB, LANES)), ("y", "x"), 0, 0, tiled=True
    )
    wide = wide.reshape(NY, NX, 4, JB, LANES).sum(1)
    totals = wide[:, 3, 0].sum(0)
    near = lax.dynamic_slice_in_dim(
        jnp.pad(wide[:, :3], ((2, 2), (0, 0), (0, 0), (0, 0))), y, 5, axis=0
    )
    own = jnp.stack([near[d, 2] + near[d + 1, 1] + near[d + 2, 0] for d in range(3)]).reshape(SLOT, LANES)
    line = lax.all_to_all(jnp.broadcast_to(own[None], (NZ, SLOT, LANES)), "z", 0, 0, tiled=True)
    full = lax.all_gather(line, "c", axis=0, tiled=False)
    return full.reshape(TABLE, LANES), totals


def sum_all(scalars):
    row = jnp.zeros((1, LANES), jnp.float32)
    for i, value in enumerate(scalars):
        row = row.at[0, i].set(value)
    count = NY * NX * NC
    row = lax.all_to_all(jnp.broadcast_to(row[None], (count, 1, LANES)), ("y", "x", "c"), 0, 0, tiled=True).sum(0)
    row = lax.all_to_all(jnp.broadcast_to(row[None], (NZ, 1, LANES)), "z", 0, 0, tiled=True).sum(0)
    return row[0]


def local(sensitivity, tile_rows, tile_cols, tile_count, travel_times):
    tiles = sensitivity[0]
    row_ids = tile_rows[0]
    column_ids = tile_cols[0]
    live_count = tile_count[0]
    slots = tiles.shape[0]
    is_live = jnp.arange(slots, dtype=jnp.int32) < live_count
    row_onehot = (row_ids[None, :] == jnp.arange(travel_times.shape[0], dtype=jnp.int32)[:, None]).astype(jnp.float32)
    y = lax.axis_index("y")
    within = column_ids % SLAB
    position = (within // JB) * SLOT + (column_ids // SLAB - y + 1) * JB + within % JB
    mine = (lax.axis_index("x") * NZ + lax.axis_index("z")) * (2 * NC) + lax.axis_index("c") * 2
    mine = (mine // JB) * SLOT + JB + mine % JB

    def forward(cells):
        picked = jnp.take(cells, position, axis=0)
        product = jnp.einsum("kij,kj->ki", tiles, picked, precision=lax.Precision.HIGHEST)
        product = jnp.where(is_live[:, None], product, jnp.float32(0.0))
        return jnp.dot(row_onehot, product, precision=lax.Precision.HIGHEST)

    def backward(rays):
        picked = jnp.take(rays, row_ids, axis=0)
        product = jnp.einsum("kij,ki->kj", tiles, picked, precision=lax.Precision.HIGHEST)
        product = jnp.where(is_live[:, None], product, jnp.float32(0.0))
        return jax.ops.segment_sum(product, position, num_segments=TABLE)

    def own(cells):
        return lax.dynamic_slice_in_dim(cells, mine, 2, axis=0)

    cells_0, total = reduce_table(backward(travel_times), [jnp.sum(travel_times * travel_times)], y)
    beta_1 = jnp.sqrt(total[0])
    ray_1 = travel_times / beta_1
    raw_1 = cells_0 / beta_1
    image_1 = forward(raw_1)
    own_raw = own(raw_1)
    cells_1, total = reduce_table(
        backward(image_1),
        [jnp.sum(own_raw * own_raw), jnp.sum(image_1 * image_1), jnp.sum(image_1 * ray_1)],
        y,
    )
    alpha_1 = jnp.sqrt(total[0])
    beta_2 = jnp.sqrt(total[1] / total[0] - 2.0 * total[2] + total[0])
    ray_2 = (image_1 / alpha_1 - alpha_1 * ray_1) / beta_2
    raw_2 = (cells_1 / alpha_1 - alpha_1 * raw_1) / beta_2 - (beta_2 / alpha_1) * raw_1
    image_2 = forward(raw_2)
    own_raw_2 = own(raw_2)
    total = sum_all(
        [jnp.sum(own_raw_2 * own_raw_2), jnp.sum(image_2 * image_2), jnp.sum(image_2 * ray_2)]
    )
    alpha_2 = jnp.sqrt(total[0])
    beta_3 = jnp.sqrt(total[1] / total[0] - 2.0 * total[2] + total[0])
    direction = own_raw / alpha_1
    rho_1 = jnp.sqrt(alpha_1 * alpha_1 + beta_2 * beta_2)
    cosine, sine = alpha_1 / rho_1, beta_2 / rho_1
    update = (cosine * beta_1 / rho_1) * direction
    phi_bar = sine * beta_1
    rho_bar = -cosine * alpha_2
    direction = own_raw_2 / alpha_2 - (sine * alpha_2 / rho_1) * direction
    rho_2 = jnp.sqrt(rho_bar * rho_bar + beta_3 * beta_3)
    cosine, sine = rho_bar / rho_2, beta_3 / rho_2
    update = update + (cosine * phi_bar / rho_2) * direction
    phi_bar = sine * phi_bar
    return update, (phi_bar / beta_1).reshape(1)


def solution(mesh):
    split = Mesh(mesh.devices.reshape(NY, NX, NZ, NC), ("y", "x", "z", "c"))
    every = P(("y", "x", "z", "c"))
    return jax.shard_map(
        local, mesh=split, in_specs=(every,) * 5, out_specs=(every, P()), check_vma=False
    )
```

time: 1050 us -> 205 us (0.20)
  waiting for transfers between devices: 522 us -> 37.1 us
  blocking collectives: 461 us -> 94.5 us
  local copies, waits for them, and re-layouts: 5.03 us -> 17.9 us
  between operations: 24.4 us -> 12.9 us
    unnamed x4 -> x0, waiting for transfers between devices: 509 us -> none
    psum x3 -> x0, blocking collectives: 330 us -> none  [the longest x2 209 us: advance(): lax.psum((jnp.sum(raw_cells * raw_cells), jnp.sum(image * image), jnp.sum...]
    all_gather x2 -> x4, blocking collectives: 131 us -> 27.1 us  [the longest x2 14.9 us: reduce_table(): pair = lax.all_gather(table, 'c', axis=0, tiled=False)]
    all_to_all x0 -> x4, blocking collectives: none -> 67.4 us  [the longest x2 33.5 us: reduce_table(): part = lax.all_to_all(half, 'z', 0, 0, tiled=True).sum(0)]
    all_to_all x0 -> x4, waiting for transfers between devices: none -> 37.1 us  [the longest x2 14.9 us: reduce_table(): lax.all_to_all(jnp.broadcast_to(own[None], (NZ, SLOT, LANES)), 'z', 0, 0,...]
    all_to_all x0 -> x4, starting transfers between devices: none -> 22.5 us  [the longest x1 9.67 us: reduce_table(): lax.all_to_all(jnp.broadcast_to(part[None], (NY * NX, SLOT + JB, LANES)),...]
    ppermute x8 -> x0, starting transfers between devices: 17.6 us -> none  [the longest x4 12.4 us: extended(): lax.ppermute(tail, axis, [(i, (i + 1) % count) for i in range(ends)])]
    ppermute x8 -> x0, waiting for transfers between devices: 13.2 us -> none  [the longest x4 13.2 us: extended(): lax.ppermute(head, axis, [((i + 1) % count, i) for i in range(ends)])]
  transfers between devices with their start and end apart: 10 -> 4, of which waited for: 6 -> 4; matrix products, arithmetic and copies ran while one was open for 0% -> 2% of each run, Pallas kernels for 0% -> 0%
where the time goes in v1:
time: 205 us; the launch traced here: 204 us
  blocking collectives  94.5 us (46%)
  waiting for transfers between devices  37.1 us (18%)
  starting transfers between devices  22.5 us (11%)
  local copies, waits for them, and re-layouts  17.9 us (9%)
  between operations  12.9 us (6%)
  other arithmetic  12 us (6%)
  matrix products  7.21 us (4%)
    all_to_all x2, blocking collectives, reduce_table(): part = lax.all_to_all(half, 'z', 0, 0, tiled=True).sum(0)  33.5 us
    all_to_all x1, blocking collectives, reduce_table(): lax.all_to_all(jnp.broadcast_to(part[None], (NY * NX, SLOT + JB, LANES)),...  19.4 us
    all_to_all x2, waiting for transfers between devices, reduce_table(): lax.all_to_all(jnp.broadcast_to(own[None], (NZ, SLOT, LANES)), 'z', 0, 0,...  14.9 us
    all_gather x2, blocking collectives, reduce_table(): pair = lax.all_gather(table, 'c', axis=0, tiled=False)  14.9 us
    all_to_all x1, blocking collectives, sum_all(): lax.all_to_all(jnp.broadcast_to(row[None], (count, 1, LANES)), ('y', 'x',...  14.5 us
    all_to_all x1, waiting for transfers between devices, reduce_table(): lax.all_to_all(jnp.broadcast_to(part[None], (NY * NX, SLOT + JB, LANES)),...  13.5 us
    all_gather x2, blocking collectives, reduce_table(): full = lax.all_gather(line, 'c', axis=0, tiled=False)  12.2 us
    all_to_all x1, starting transfers between devices, reduce_table(): lax.all_to_all(jnp.broadcast_to(part[None], (NY * NX, SLOT + JB, LANES)),...  9.67 us
  transfers between devices with their start and end apart: 4, of which 4 were waited for; matrix products, arithmetic and copies ran while one was open for 2% of the time, Pallas kernels for 0%

profile of v1, /device:TPU:1, one launch (start us, length us, event | category | flops | bytes accessed | tf_op | source)
XLA Modules:
  0.0 204.1 jit_solution(3423971858512302740)
XLA Ops:
  6.0 12.5 %all-gather = f32[4,12,32,128]{3,2,1,0:T(8,128)S(1)} all-gather(f32[2,12,32,128]{3,2,1,0:T(8,128)S(1)} %pad_maximum_fusion), channel_id=2, replica_groups=mesh['y'=8,'x'=4,'z'=12,'c'=2] {'c'}, dimensions={0}, use_global_device_ids=true | all-gather | bytes 1179648 | tf_op jit(solution)/shard_map/all_gather | solution.py:21
  18.5 18.3 %all_to_all.40 = f32[12,32,128]{2,1,0:T(8,128)S(1)} all-to-all(f32[12,32,128]{2,1,0:T(8,128)S(1)} %dynamic-slice_reduce_fusion.1), channel_id=1, replica_groups=mesh['y'=8,'x'=4,'z'=12,'c'=2] {'z'}, dimensions={0} | all-to-all | bytes 393216 | tf_op jit(solution)/shard_map/all_to_all | solution.py:23
  37.6 9.7 %all-to-all-start.1 = ((f32[32,32,128]{2,1,0:T(8,128)}), f32[32,32,128]{2,1,0:T(8,128)S(1)}, u32[]{:S(2)}, u32[]{:S(2)}) async-start(f32[32,32,128]{2,1,0:T(8,128)} %broadcast_in_dim.101), calls=%async_computation.1 | async-start | bytes 1048576 | tf_op jit(solution)/shard_map/all_to_all | solution.py:24
  48.1 13.5 %all-to-all-done.1 = f32[32,32,128]{2,1,0:T(8,128)S(1)} async-done(((f32[32,32,128]{2,1,0:T(8,128)}), f32[32,32,128]{2,1,0:T(8,128)S(1)}, u32[]{:S(2)}, u32[]{:S(2)}) %all-to-all-start.1) | async-done | bytes 524320 | tf_op jit(solution)/shard_map/all_to_all | solution.py:24
  62.4 5.2 %all-to-all-start.2 = ((f32[12,24,128]{2,1,0:T(8,128)}), f32[12,24,128]{2,1,0:T(8,128)S(1)}, u32[]{:S(2)}, u32[]{:S(2)}) async-start(f32[12,24,128]{2,1,0:T(8,128)} %broadcast_in_dim.103), calls=%async_computation.2 | async-start | bytes 294912 | tf_op jit(solution)/shard_map/all_to_all | solution.py:33
  69.0 9.3 %all-to-all-done.2 = f32[12,24,128]{2,1,0:T(8,128)S(1)} async-done(((f32[12,24,128]{2,1,0:T(8,128)}), f32[12,24,128]{2,1,0:T(8,128)S(1)}, u32[]{:S(2)}, u32[]{:S(2)}) %all-to-all-start.2) | async-done | bytes 147488 | tf_op jit(solution)/shard_map/all_to_all | solution.py:33
  78.3 6.1 %all-gather.1 = f32[24,24,128]{2,1,0:T(8,128)S(1)} all-gather(f32[12,24,128]{2,1,0:T(8,128)S(1)} %all-to-all-done.2), channel_id=3, replica_groups=mesh['y'=8,'x'=4,'z'=12,'c'=2] {'c'}, dimensions={0}, use_global_device_ids=true | all-gather | bytes 442368 | tf_op jit(solution)/shard_map/all_gather | solution.py:34
  85.1 1.7 fusion.4
  91.4 2.0 scatter.26
  93.4 1.9 dynamic-slice.51
  97.2 1.4 scatter.29
  98.7 2.4 %all-gather.2 = f32[4,12,32,128]{3,2,1,0:T(8,128)S(1)} all-gather(f32[2,12,32,128]{3,2,1,0:T(8,128)S(1)} %pad_maximum_fusion.1), channel_id=4, replica_groups=mesh['y'=8,'x'=4,'z'=12,'c'=2] {'c'}, dimensions={0}, use_global_device_ids=true | all-gather | bytes 1179648 | tf_op jit(solution)/shard_map/all_gather | solution.py:21
  101.1 15.3 %all_to_all.41 = f32[12,32,128]{2,1,0:T(8,128)S(1)} all-to-all(f32[12,32,128]{2,1,0:T(8,128)S(1)} %dynamic-slice_reduce_fusion), channel_id=1, replica_groups=mesh['y'=8,'x'=4,'z'=12,'c'=2] {'z'}, dimensions={0} | all-to-all | bytes 393216 | tf_op jit(solution)/shard_map/all_to_all | solution.py:23
  116.5 19.4 %all_to_all.42 = f32[32,32,128]{2,1,0:T(8,128)S(1)} all-to-all(f32[32,32,128]{2,1,0:T(8,128)S(1)} %broadcast_in_dim.105), channel_id=1, replica_groups=mesh['y'=8,'x'=4,'z'=12,'c'=2] {'y','x'}, dimensions={0} | all-to-all | bytes 1048576 | tf_op jit(solution)/shard_map/all_to_all | solution.py:24
  136.7 4.2 %all-to-all-start.5 = ((f32[12,24,128]{2,1,0:T(8,128)}), f32[12,24,128]{2,1,0:T(8,128)S(1)}, u32[]{:S(2)}, u32[]{:S(2)}) async-start(f32[12,24,128]{2,1,0:T(8,128)} %broadcast_in_dim.107), calls=%async_computation.5 | async-start | bytes 294912 | tf_op jit(solution)/shard_map/all_to_all | solution.py:33
  146.0 5.6 %all-to-all-done.5 = f32[12,24,128]{2,1,0:T(8,128)S(1)} async-done(((f32[12,24,128]{2,1,0:T(8,128)}), f32[12,24,128]{2,1,0:T(8,128)S(1)}, u32[]{:S(2)}, u32[]{:S(2)}) %all-to-all-start.5) | async-done | bytes 147488 | tf_op jit(solution)/shard_map/all_to_all | solution.py:33
  151.6 6.1 %all-gather.3 = f32[24,24,128]{2,1,0:T(8,128)S(1)} all-gather(f32[12,24,128]{2,1,0:T(8,128)S(1)} %all-to-all-done.5), channel_id=5, replica_groups=mesh['y'=8,'x'=4,'z'=12,'c'=2] {'c'}, dimensions={0}, use_global_device_ids=true | all-gather | bytes 442368 | tf_op jit(solution)/shard_map/all_gather | solution.py:34
  159.1 1.7 fusion
  163.0 2.5 %fusion.59 = f32[1,1]{1,0:T(1,128)} fusion(pred[1,1]{1,0:T(4,128)(4,1)} %bitcast.52, f32[1,1]{1,0:T(1,128)} %bitcast.57, s32[]{:T(128)} %bitcast.36, f32[1,1]{1,0:T(1,128)} %bitcast.51), kind=kLoop, calls=%fused_computation.142 | loop fusion | flops 1 | bytes 17 | tf_op jit(solution)/shard_map/select.12
  165.5 1.4 scatter.31
  166.9 2.6 %fusion.60 = f32[1,1]{1,0:T(1,128)} fusion(pred[1,1]{1,0:T(4,128)(4,1)} %bitcast.59, f32[1,1]{1,0:T(1,128)} %bitcast.60, f32[1,128]{1,0:T(1,128)S(1)} %scatter.31, s32[]{:T(128)} %bitcast.40), kind=kLoop, calls=%fused_computation.143 | loop fusion | flops 1 | bytes 17 | tf_op jit(solution)/shard_map/select.13
  170.9 14.5 %all_to_all.43 = f32[64,1,128]{2,1,0:T(1,128)S(1)} all-to-all(f32[64,1,128]{2,1,0:T(1,128)S(1)} %broadcast_in_dim.110), channel_id=1, replica_groups=mesh['y'=8,'x'=4,'z'=12,'c'=2] {'y','x','c'}, dimensions={0} | all-to-all | bytes 65536 | tf_op jit(solution)/shard_map/all_to_all | solution.py:43
  186.0 3.5 %all-to-all-start.7 = ((f32[12,1,128]{2,1,0:T(1,128)}), f32[12,1,128]{2,1,0:T(1,128)S(1)}, u32[]{:S(2)}, u32[]{:S(2)}) async-start(f32[12,1,128]{2,1,0:T(1,128)} %broadcast_in_dim.111), calls=%async_computation.7 | async-start | bytes 12288 | tf_op jit(solution)/shard_map/all_to_all | solution.py:44
  189.7 8.6 %all-to-all-done.7 = f32[12,1,128]{2,1,0:T(1,128)S(1)} async-done(((f32[12,1,128]{2,1,0:T(1,128)}), f32[12,1,128]{2,1,0:T(1,128)S(1)}, u32[]{:S(2)}, u32[]{:S(2)}) %all-to-all-start.7) | async-done | bytes 6176 | tf_op jit(solution)/shard_map/all_to_all | solution.py:44
  (77 shorter events, 21.9 us)
Async XLA Ops:
  0.6 2.8 %copy-start = (f32[1,16,128,128]{3,2,1,0:T(8,128)S(1)}, f32[1,16,128,128]{3,2,1,0:T(8,128)}, u32[]{:S(2)}) copy-start(f32[1,16,128,128]{3,2,1,0:T(8,128)} %param.23) | copy-start | bytes 3145732
  0.6 0.7 copy-start.3
  1.4 0.7 copy-start.1
  2.7 0.7 copy-start.2
  37.6 24.0 %all-to-all-start.1 = ((f32[32,32,128]{2,1,0:T(8,128)}), f32[32,32,128]{2,1,0:T(8,128)S(1)}, u32[]{:S(2)}, u32[]{:S(2)}) async-start(f32[32,32,128]{2,1,0:T(8,128)} %broadcast_in_dim.101), calls=%async_computation.1 | async-start | bytes 1048576 | tf_op jit(solution)/shard_map/all_to_all | solution.py:24
  62.4 15.9 %all-to-all-start.2 = ((f32[12,24,128]{2,1,0:T(8,128)}), f32[12,24,128]{2,1,0:T(8,128)S(1)}, u32[]{:S(2)}, u32[]{:S(2)}) async-start(f32[12,24,128]{2,1,0:T(8,128)} %broadcast_in_dim.103), calls=%async_computation.2 | async-start | bytes 294912 | tf_op jit(solution)/shard_map/all_to_all | solution.py:33
  67.6 0.7 copy-start.4
  136.7 14.9 %all-to-all-start.5 = ((f32[12,24,128]{2,1,0:T(8,128)}), f32[12,24,128]{2,1,0:T(8,128)S(1)}, u32[]{:S(2)}, u32[]{:S(2)}) async-start(f32[12,24,128]{2,1,0:T(8,128)} %broadcast_in_dim.107), calls=%async_computation.5 | async-start | bytes 294912 | tf_op jit(solution)/shard_map/all_to_all | solution.py:33
  186.0 12.3 %all-to-all-start.7 = ((f32[12,1,128]{2,1,0:T(1,128)}), f32[12,1,128]{2,1,0:T(1,128)S(1)}, u32[]{:S(2)}, u32[]{:S(2)}) async-start(f32[12,1,128]{2,1,0:T(1,128)} %broadcast_in_dim.111), calls=%async_computation.7 | async-start | bytes 12288 | tf_op jit(solution)/shard_map/all_to_all | solution.py:44

commit v2 on v1

v2 whole, which is shorter than its diff:
```python
import jax
import jax.numpy as jnp
from jax import lax
from jax.experimental import pallas as pl
from jax.experimental.pallas import tpu as pltpu
from jax.sharding import Mesh, PartitionSpec as P

NY, NX, NZ, NC = 8, 4, 12, 2
SLAB = 192
JB = SLAB // (NC * NZ)
SLOT = 3 * JB
WIDE = SLOT + JB
LANES = 128
TABLE = NC * NZ * SLOT
TS = 16
RB = 16
VM = pl.BlockSpec(memory_space=pltpu.VMEM)
SM = pl.BlockSpec(memory_space=pltpu.SMEM)


def shape(*dims):
    return jax.ShapeDtypeStruct(dims, jnp.float32)


def call(kernel, outs, ins, args, scratch=()):
    return pl.pallas_call(
        kernel,
        out_shape=outs,
        in_specs=ins,
        out_specs=jax.tree.map(lambda _: VM, outs),
        scratch_shapes=scratch,
        compiler_params=pltpu.CompilerParams(vmem_limit_bytes=32 * 1024 * 1024),
    )(*args)


def live(ids, k):
    return jnp.where(k < ids[3, 0], jnp.float32(1.0), jnp.float32(0.0))


def total(value):
    return jnp.sum(jnp.sum(value, axis=0, keepdims=True), axis=1, keepdims=True)


def packed(values):
    lane = lax.broadcasted_iota(jnp.int32, (1, LANES), 1)
    row = jnp.zeros((1, LANES), jnp.float32)
    for i, value in enumerate(values):
        row = jnp.where(lane == i, value, row)
    return row


def backward_terms(ids, tiles, columns, table, where):
    for k in range(TS):
        term = jnp.sum(tiles[k] * columns[ids[0, k]], axis=0, keepdims=True) * live(ids, k)
        at = pl.ds(ids[where, k], 1)
        table[at, :] = table[at, :] + term


def first_kernel(ids, tiles, times, table, times_t, columns):
    padded = jnp.concatenate([times[...], jnp.zeros((LANES - RB, LANES), jnp.float32)], axis=0)
    turned = padded.T
    times_t[...] = turned
    for r in range(RB):
        columns[r] = jnp.broadcast_to(turned[:, r : r + 1], (LANES, LANES))
    table[...] = jnp.zeros_like(table)
    backward_terms(ids, tiles, columns, table, 1)


def second_kernel(ids, tiles, cells, times_t, table, image_t, columns):
    columns[...] = jnp.zeros_like(columns)
    for k in range(TS):
        term = jnp.sum(tiles[k] * cells[pl.ds(ids[1, k], 1), :], axis=1, keepdims=True) * live(ids, k)
        r = ids[0, k]
        columns[r] = columns[r] + term
    lane = lax.broadcasted_iota(jnp.int32, (LANES, LANES), 1)
    image = jnp.zeros((LANES, LANES), jnp.float32)
    for r in range(RB):
        image = jnp.where(lane == r, columns[r], image)
    image_t[...] = image
    table[...] = jnp.zeros_like(table)
    backward_terms(ids, tiles, columns, table, 2)
    times = times_t[...]
    own = cells[pl.ds(ids[3, 1], 2), :]
    row = packed([total(times * times), total(own * own), total(image * image), total(image * times)])
    for s in range(NC * NZ):
        table[s * WIDE + SLOT : s * WIDE + SLOT + 1, :] = row


def norms(sums):
    times_2, cells_2, image_2, cross = (sums[:, i : i + 1] for i in range(4))
    beta_1 = jnp.sqrt(times_2)
    square = cells_2 / times_2
    alpha_1 = jnp.sqrt(square)
    beta_2 = jnp.sqrt(image_2 / cells_2 - 2.0 * (cross / times_2) + square)
    return beta_1, alpha_1, beta_2


def third_kernel(ids, tiles, cells, cells_2, times_t, image_t, sums, rows, own_raw):
    beta_1, alpha_1, beta_2 = norms(sums[...])
    scale = 1.0 / (beta_1 * alpha_1 * beta_2)
    shift = (alpha_1 / beta_2 + beta_2 / alpha_1) / beta_1
    lane = lax.broadcasted_iota(jnp.int32, (LANES, LANES), 1)
    image = jnp.zeros((LANES, LANES), jnp.float32)
    for k in range(TS):
        at = pl.ds(ids[1, k], 1)
        raw = scale * cells_2[at, :] - shift * cells[at, :]
        term = jnp.sum(tiles[k] * raw, axis=1, keepdims=True) * live(ids, k)
        image = image + jnp.where(lane == ids[0, k], term, 0.0)
    ray = (image_t[...] / (alpha_1 * beta_1) - (alpha_1 / beta_1) * times_t[...]) / beta_2
    at = pl.ds(ids[3, 1], 2)
    own_1 = cells[at, :]
    own_2 = scale * cells_2[at, :] - shift * own_1
    own_raw[0] = own_1 / beta_1
    own_raw[1] = own_2
    row = packed([total(own_2 * own_2), total(image * image), total(image * ray)])
    rows[...] = jnp.broadcast_to(row[None], rows.shape)


def last_kernel(rows, sums, own_raw, update, ratio):
    beta_1, alpha_1, beta_2 = norms(sums[...])
    row = jnp.sum(rows[...], axis=0)
    cells_2, image_2, cross = (row[:, i : i + 1] for i in range(3))
    alpha_2 = jnp.sqrt(cells_2)
    beta_3 = jnp.sqrt(image_2 / cells_2 - 2.0 * cross + cells_2)
    direction = own_raw[0] / alpha_1
    rho_1 = jnp.sqrt(alpha_1 * alpha_1 + beta_2 * beta_2)
    cosine, sine = alpha_1 / rho_1, beta_2 / rho_1
    found = (cosine * beta_1 / rho_1) * direction
    phi_bar = sine * beta_1
    rho_bar = -cosine * alpha_2
    direction = own_raw[1] / alpha_2 - (sine * alpha_2 / rho_1) * direction
    rho_2 = jnp.sqrt(rho_bar * rho_bar + beta_3 * beta_3)
    cosine, sine = rho_bar / rho_2, beta_3 / rho_2
    update[...] = found + (cosine * phi_bar / rho_2) * direction
    ratio[...] = sine * phi_bar / beta_1


def line_kernel(parts, copies):
    total_part = parts[0]
    for z in range(1, NZ):
        total_part = total_part + parts[z]
    for s in range(NY * NX):
        copies[s] = total_part


def plane_kernel(ids, parts, copies, *sums):
    y = ids[3, 2]
    for d in range(3):
        acc = jnp.zeros((JB, LANES), jnp.float32)
        for e in range(3):
            other = y + (d - 1) + (e - 1)
            inside = jnp.logical_and(other >= 0, other < NY)
            base = jnp.clip(other, 0, NY - 1) * NX
            rel = 2 - e
            term = parts[base, rel * JB : (rel + 1) * JB, :]
            for x in range(1, NX):
                term = term + parts[base + x, rel * JB : (rel + 1) * JB, :]
            acc = acc + jnp.where(inside, term, 0.0)
        for z in range(NZ):
            copies[z, d * JB : (d + 1) * JB, :] = acc
    if sums:
        row = parts[0, SLOT : SLOT + 1, :]
        for s in range(1, NY * NX):
            row = row + parts[s, SLOT : SLOT + 1, :]
        sums[0][...] = row


def exchange(table, ids, depth):
    core = lax.axis_index("c")
    pair = lax.all_gather(table.reshape(NC, NZ, depth, LANES), "c", axis=0, tiled=False)
    half = lax.dynamic_index_in_dim(pair, core, axis=1, keepdims=False).sum(0)
    parts = lax.all_to_all(half, "z", 0, 0, tiled=True)
    copies = call(line_kernel, shape(NY * NX, depth, LANES), [VM], (parts,))
    parts = lax.all_to_all(copies, ("y", "x"), 0, 0, tiled=True)
    outs = [shape(NZ, SLOT, LANES)] + ([shape(1, LANES)] if depth > SLOT else [])
    copies, *sums = call(plane_kernel, outs, [SM, VM], (ids, parts))
    line = lax.all_to_all(copies, "z", 0, 0, tiled=True)
    full = lax.all_gather(line, "c", axis=0, tiled=False)
    return full.reshape(TABLE, LANES), *sums


def local(sensitivity, tile_rows, tile_cols, tile_count, travel_times):
    tiles = sensitivity[0]
    columns = tile_cols[0]
    y = lax.axis_index("y")
    within = columns % SLAB
    slot = within // JB
    offset = jnp.clip(columns // SLAB - y + 1, 0, 2) * JB + within % JB
    mine = (lax.axis_index("x") * NZ + lax.axis_index("z")) * (2 * NC) + lax.axis_index("c") * 2
    mine = (mine // JB) * SLOT + JB + mine % JB
    place = jnp.arange(TS, dtype=jnp.int32)
    facts = jnp.where(place == 0, tile_count[0], jnp.where(place == 1, mine, y))
    ids = jnp.stack([jnp.clip(tile_rows[0], 0, RB - 1), slot * SLOT + offset, slot * WIDE + offset, facts])
    square = shape(LANES, LANES)
    scratch = [pltpu.VMEM((RB, LANES, LANES), jnp.float32)]

    table, times_t = call(
        first_kernel, [shape(TABLE, LANES), square], [SM, VM, VM], (ids, tiles, travel_times), scratch
    )
    (cells,) = exchange(table, ids, SLOT)
    table, image_t = call(
        second_kernel,
        [shape(NC * NZ * WIDE, LANES), square],
        [SM, VM, VM, VM],
        (ids, tiles, cells, times_t),
        scratch,
    )
    cells_2, sums = exchange(table, ids, WIDE)
    count = NY * NX * NC
    rows, own_raw = call(
        third_kernel,
        [shape(count, 1, LANES), shape(2, 2, LANES)],
        [SM] + [VM] * 6,
        (ids, tiles, cells, cells_2, times_t, image_t, sums),
    )
    rows = lax.all_to_all(rows, ("y", "x", "c"), 0, 0, tiled=True)
    rows = jnp.broadcast_to(rows.sum(0)[None], (NZ, 1, LANES))
    rows = lax.all_to_all(rows, "z", 0, 0, tiled=True)
    update, ratio = call(last_kernel, [shape(2, LANES), shape(1, 1)], [VM] * 3, (rows, sums, own_raw))
    return update, ratio.reshape(1)


def solution(mesh):
    split = Mesh(mesh.devices.reshape(NY, NX, NZ, NC), ("y", "x", "z", "c"))
    every = P(("y", "x", "z", "c"))
    return jax.shard_map(
        local, mesh=split, in_specs=(every,) * 5, out_specs=(every, P()), check_vma=False
    )
```

time: 205 us -> 167 us (0.81)
  blocking collectives: 94.5 us -> 156 us
  waiting for transfers between devices: 37.1 us -> 0 us
  starting transfers between devices: 22.5 us -> 0 us
  local copies, waits for them, and re-layouts: 17.9 us -> 2.56 us
  other arithmetic: 12 us -> 0.17 us
  between operations: 12.9 us -> 1.47 us
  matrix products: 7.21 us -> 0 us
  Pallas kernels: 0 us -> 5.98 us
    all_to_all x4 -> x8, blocking collectives: 67.4 us -> 129 us  [the longest x2 40.8 us: exchange(): parts = lax.all_to_all(copies, ('y', 'x'), 0, 0, tiled=True)]
    all_to_all x4 -> x0, waiting for transfers between devices: 37.1 us -> none  [the longest x2 14.9 us: reduce_table(): lax.all_to_all(jnp.broadcast_to(own[None], (NZ, SLOT, LANES)), 'z', 0, 0,...]
    all_to_all x4 -> x0, starting transfers between devices: 22.5 us -> none  [the longest x1 9.67 us: reduce_table(): lax.all_to_all(jnp.broadcast_to(part[None], (NY * NX, SLOT + JB, LANES)),...]
    scatter x7 -> x0, local copies, waits for them, and re-layouts: 7.49 us -> none  [the longest x4 4.7 us: reduce_table(): row = row.at[0, i].set(value)]
    dot_general x6 -> x0, matrix products: 7.21 us -> none  [the longest x2 3.46 us: forward(): jnp.einsum('kij,kj->ki', tiles, picked, precision=lax.Precision.HIGHEST)]
    another operation x6 -> x1, other arithmetic: 7.11 us -> 0.01 us  [local(): jnp.stack([jnp.clip(tile_rows[0], 0, RB - 1), slot * SLOT + offset, slot...]
    pallas_call x0 -> x8, Pallas kernels: none -> 5.98 us  [call(): pl.pallas_call(kernel, out_shape=outs, in_specs=ins, out_specs=jax.tree.m...]
    another operation x4 -> x0, local copies, waits for them, and re-layouts: 3.21 us -> none
  transfers between devices with their start and end apart: 4 -> 0, of which waited for: 4 -> 0; matrix products, arithmetic and copies ran while one was open for 2% -> 0% of each run, Pallas kernels for 0% -> 0%
where the time goes in v2:
time: 167 us; the launch traced here: 166 us
  blocking collectives  156 us (93%)
  Pallas kernels  5.98 us (4%)
  local copies, waits for them, and re-layouts  2.56 us (2%)
    all_to_all x2, blocking collectives, exchange(): parts = lax.all_to_all(copies, ('y', 'x'), 0, 0, tiled=True)  40.8 us
    all_to_all x2, blocking collectives, exchange(): parts = lax.all_to_all(half, 'z', 0, 0, tiled=True)  32.3 us
    all_to_all x2, blocking collectives, exchange(): line = lax.all_to_all(copies, 'z', 0, 0, tiled=True)  30.6 us
    all_gather x2, blocking collectives, exchange(): lax.all_gather(table.reshape(NC, NZ, depth, LANES), 'c', axis=0, tiled=Fa...  14.7 us
    all_to_all x1, blocking collectives, local(): rows = lax.all_to_all(rows, ('y', 'x', 'c'), 0, 0, tiled=True)  14.5 us
    all_gather x2, blocking collectives, exchange(): full = lax.all_gather(line, 'c', axis=0, tiled=False)  11.7 us
    all_to_all x1, blocking collectives, local(): rows = lax.all_to_all(rows, 'z', 0, 0, tiled=True)  11.4 us
    pallas_call x8, Pallas kernels, call(): pl.pallas_call(kernel, out_shape=outs, in_specs=ins, out_specs=jax.tree.m...  5.98 us

profile of v2, /device:TPU:1, one launch (start us, length us, event | category | flops | bytes accessed | tf_op | source)
XLA Modules:
  0.0 166.1 jit_solution(10068129400956615017)
XLA Ops:
  1.4 0.0 copy-start.3
  1.4 0.6 copy-done.3
  2.1 0.7 copy-done.2
  2.8 1.2 copy-done
  4.0 1.2 shard_map.68
  5.2 12.4 %all_gather.18 = f32[2,2,12,24,128]{4,3,2,1,0:T(8,128)S(1)} all-gather(f32[1,2,12,24,128]{4,3,2,1,0:T(8,128)S(1)} %bitcast.15), channel_id=1, replica_groups=mesh['y'=8,'x'=4,'z'=12,'c'=2] {'c'}, dimensions={0}, use_global_device_ids=true | all-gather | bytes 884736 | tf_op jit(solution)/shard_map/all_gather | solution.py:170
  17.6 17.0 %all_to_all.40.parts = f32[12,24,128]{2,1,0:T(8,128)S(1)} all-to-all(f32[12,24,128]{2,1,0:T(8,128)S(1)} %dynamic-slice_reduce_fusion.1), channel_id=1, replica_groups=mesh['y'=8,'x'=4,'z'=12,'c'=2] {'z'}, dimensions={0} | all-to-all | bytes 294912 | tf_op jit(solution)/shard_map/all_to_all | solution.py:172
  34.6 21.1 %all_to_all.41.parts = f32[32,24,128]{2,1,0:T(8,128)S(1)} all-to-all(f32[32,24,128]{2,1,0:T(8,128)S(1)} %shard_map.69), channel_id=1, replica_groups=mesh['y'=8,'x'=4,'z'=12,'c'=2] {'y','x'}, dimensions={0} | all-to-all | bytes 786432 | tf_op jit(solution)/shard_map/all_to_all | solution.py:174
  55.8 0.6 shard_map.70
  56.4 16.3 %all_to_all.42 = f32[12,24,128]{2,1,0:T(8,128)S(1)} all-to-all(f32[12,24,128]{2,1,0:T(8,128)S(1)} %shard_map.70), channel_id=1, replica_groups=mesh['y'=8,'x'=4,'z'=12,'c'=2] {'z'}, dimensions={0} | all-to-all | bytes 294912 | tf_op jit(solution)/shard_map/all_to_all | solution.py:177
  72.7 5.6 %all-gather = f32[24,24,128]{2,1,0:T(8,128)S(1)} all-gather(f32[12,24,128]{2,1,0:T(8,128)S(1)} %all_to_all.42), channel_id=2, replica_groups=mesh['y'=8,'x'=4,'z'=12,'c'=2] {'c'}, dimensions={0}, use_global_device_ids=true | all-gather | bytes 442368 | tf_op jit(solution)/shard_map/all_gather | solution.py:178
  78.3 1.2 shard_map.71
  79.5 2.4 %all_gather.21 = f32[2,2,12,32,128]{4,3,2,1,0:T(8,128)S(1)} all-gather(f32[1,2,12,32,128]{4,3,2,1,0:T(8,128)S(1)} %bitcast.14), channel_id=1, replica_groups=mesh['y'=8,'x'=4,'z'=12,'c'=2] {'c'}, dimensions={0}, use_global_device_ids=true | all-gather | bytes 1179648 | tf_op jit(solution)/shard_map/all_gather | solution.py:170
  81.9 15.3 %all_to_all.43.parts = f32[12,32,128]{2,1,0:T(8,128)S(1)} all-to-all(f32[12,32,128]{2,1,0:T(8,128)S(1)} %dynamic-slice_reduce_fusion), channel_id=1, replica_groups=mesh['y'=8,'x'=4,'z'=12,'c'=2] {'z'}, dimensions={0} | all-to-all | bytes 393216 | tf_op jit(solution)/shard_map/all_to_all | solution.py:172
  97.2 0.1 shard_map.72
  97.2 19.6 %all_to_all.44.parts = f32[32,32,128]{2,1,0:T(8,128)S(1)} all-to-all(f32[32,32,128]{2,1,0:T(8,128)S(1)} %shard_map.72), channel_id=1, replica_groups=mesh['y'=8,'x'=4,'z'=12,'c'=2] {'y','x'}, dimensions={0} | all-to-all | bytes 1048576 | tf_op jit(solution)/shard_map/all_to_all | solution.py:174
  116.8 0.6 shard_map.73
  117.4 14.2 %all_to_all.45 = f32[12,24,128]{2,1,0:T(8,128)S(1)} all-to-all(f32[12,24,128]{2,1,0:T(8,128)S(1)} %get-tuple-element.15), channel_id=1, replica_groups=mesh['y'=8,'x'=4,'z'=12,'c'=2] {'z'}, dimensions={0} | all-to-all | bytes 294912 | tf_op jit(solution)/shard_map/all_to_all | solution.py:177
  131.7 6.1 %all-gather.1 = f32[24,24,128]{2,1,0:T(8,128)S(1)} all-gather(f32[12,24,128]{2,1,0:T(8,128)S(1)} %all_to_all.45), channel_id=3, replica_groups=mesh['y'=8,'x'=4,'z'=12,'c'=2] {'c'}, dimensions={0}, use_global_device_ids=true | all-gather | bytes 442368 | tf_op jit(solution)/shard_map/all_gather | solution.py:178
  137.8 1.3 shard_map.74
  139.1 14.5 %all_to_all.46 = f32[64,1,128]{2,1,0:T(1,128)S(1)} all-to-all(f32[64,1,128]{2,1,0:T(1,128)S(1)} %get-tuple-element.18), channel_id=1, replica_groups=mesh['y'=8,'x'=4,'z'=12,'c'=2] {'y','x','c'}, dimensions={0} | all-to-all | bytes 65536 | tf_op jit(solution)/shard_map/all_to_all | solution.py:216
  153.6 0.1 reduce_sum.29
  153.7 11.4 %all_to_all.47.rows = f32[12,1,128]{2,1,0:T(1,128)S(1)} all-to-all(f32[12,1,128]{2,1,0:T(1,128)S(1)} %broadcast_in_dim.18), channel_id=1, replica_groups=mesh['y'=8,'x'=4,'z'=12,'c'=2] {'z'}, dimensions={0} | all-to-all | bytes 12288 | tf_op jit(solution)/shard_map/all_to_all | solution.py:218
  165.1 1.0 shard_map.75
  (14 shorter events, 0.2 us)
Async XLA Ops:
  0.7 0.7 copy-start.4
  1.4 0.7 copy-start.3
  2.1 0.7 copy-start.2
  2.8 1.2 copy-start
  34.6 43.7 %copy-start.1 = (f32[1,16,128,128]{3,2,1,0:T(8,128)S(1)}, f32[1,16,128,128]{3,2,1,0:T(8,128)}, u32[]{:S(2)}) copy-start(f32[1,16,128,128]{3,2,1,0:T(8,128)} %param.5) | copy-start | bytes 3145732

commit v3 on v2

v3 whole, which is shorter than its diff:
```python
import jax
import jax.numpy as jnp
from jax import lax
from jax.experimental import pallas as pl
from jax.experimental.pallas import tpu as pltpu
from jax.sharding import Mesh, PartitionSpec as P

NY, NX, NZ, NC = 8, 4, 12, 2
NH = 2
SLAB = 192
SLOTS = NH * NZ
JB = SLAB // (NC * SLOTS)
SLOT = 3 * JB
DEPTH = 4 * JB
LANES = 128
TABLE = NC * SLOTS * DEPTH
TS = 16
RB = 16
VM = pl.BlockSpec(memory_space=pltpu.VMEM)
SM = pl.BlockSpec(memory_space=pltpu.SMEM)


def shape(*dims):
    return jax.ShapeDtypeStruct(dims, jnp.float32)


def call(kernel, outs, ins, args, scratch=()):
    return pl.pallas_call(
        kernel,
        out_shape=outs,
        in_specs=ins,
        out_specs=jax.tree.map(lambda _: VM, outs),
        scratch_shapes=scratch,
        compiler_params=pltpu.CompilerParams(vmem_limit_bytes=32 * 1024 * 1024),
    )(*args)


def coordinates():
    me = lax.axis_index("all")
    y = me // (NX * NZ * NC)
    rest = me - y * (NX * NZ * NC)
    return y, rest // NC, rest % NC


def device(y, x, z, c):
    return ((y * NX + x) * NZ + z) * NC + c


PAIRS = [[device(y, x, z, 0), device(y, x, z, 1)] for y in range(NY) for x in range(NX) for z in range(NZ)]
LINES = [
    [device(y, x, z, c) for x in pair for z in range(NZ)]
    for y in range(NY)
    for pair in ((0, 1), (3, 2))
    for c in range(NC)
]
PLANES = [
    [device(y, x, z, c) for x in pair for y in range(NY)]
    for z in range(NZ)
    for pair in ((0, 3), (1, 2))
    for c in range(NC)
]
CHIPS_Z = [
    [device(y, x, z, c) for z in range(NZ) for c in range(NC)] for y in range(NY) for x in range(NX)
]
ALL_YX = [
    [device(y, x, z, c) for y in range(NY) for x in range(NX)] for z in range(NZ) for c in range(NC)
]


def swap(array, groups):
    return lax.all_to_all(array, "all", 0, 0, tiled=True, axis_index_groups=groups)


def placed(k, rows, cols, count):
    y, _, _ = coordinates()
    column = cols[0, k]
    region = column // SLAB
    within = column - region * SLAB
    slot = within // JB
    band = jnp.clip(region - y + 1, 0, 2)
    at = jnp.clip(slot * DEPTH + band * JB + (within - slot * JB), 0, TABLE - 1)
    return jnp.clip(rows[0, k], 0, RB - 1), at, jnp.where(k < count[0], jnp.float32(1.0), jnp.float32(0.0))


def own_rows(cells):
    _, slot, core = coordinates()
    return cells[pl.ds(slot * DEPTH + JB + core * 2, 2), :]


def total(value):
    return jnp.sum(jnp.sum(value, axis=0, keepdims=True), axis=1, keepdims=True)


def packed(values):
    lane = lax.broadcasted_iota(jnp.int32, (1, LANES), 1)
    row = jnp.zeros((1, LANES), jnp.float32)
    for i, value in enumerate(values):
        row = jnp.where(lane == i, value, row)
    return row


def backward_terms(places, tiles, columns, table, row):
    spare = jnp.broadcast_to(row, (JB, LANES))
    block = jnp.concatenate([jnp.zeros((SLOT, LANES), jnp.float32), spare], axis=0)
    for s in range(NC * SLOTS):
        table[s * DEPTH : (s + 1) * DEPTH, :] = block
    for k, (r, at, weight) in enumerate(places):
        term = jnp.sum(tiles[k] * columns[r], axis=0, keepdims=True) * weight
        table[pl.ds(at, 1), :] = table[pl.ds(at, 1), :] + term


def first_kernel(rows, cols, count, tiles_far, times, table, times_t, columns, tiles, sem):
    copy = pltpu.make_async_copy(tiles_far, tiles, sem)
    copy.start()
    padded = jnp.concatenate([times[...], jnp.zeros((LANES - RB, LANES), jnp.float32)], axis=0)
    turned = padded.T
    times_t[...] = turned
    for r in range(RB):
        columns[r] = jnp.broadcast_to(turned[:, r : r + 1], (LANES, LANES))
    places = [placed(k, rows, cols, count) for k in range(TS)]
    copy.wait()
    backward_terms(places, tiles, columns, table, packed([total(turned * turned)]))


def second_kernel(rows, cols, count, tiles, cells, times_t, sums, table, image_t, columns):
    inverse = 1.0 / jnp.sqrt(sums[:, 0:1])
    places = [placed(k, rows, cols, count) for k in range(TS)]
    columns[...] = jnp.zeros_like(columns)
    for k, (r, at, weight) in enumerate(places):
        raw = cells[pl.ds(at, 1), :] * inverse
        term = jnp.sum(tiles[k] * raw, axis=1, keepdims=True) * weight
        columns[r] = columns[r] + term
    lane = lax.broadcasted_iota(jnp.int32, (LANES, LANES), 1)
    image = jnp.zeros((LANES, LANES), jnp.float32)
    for r in range(RB):
        image = jnp.where(lane == r, columns[r], image)
    image_t[...] = image
    ray = times_t[...] * inverse
    own = own_rows(cells) * inverse
    row = packed([total(own * own), total(image * image), total(image * ray)])
    backward_terms(places, tiles, columns, table, row)


def norms(sums):
    square, image_2, cross = (sums[:, i : i + 1] for i in range(3))
    return jnp.sqrt(square), jnp.sqrt(image_2 / square - 2.0 * cross + square)


def third_kernel(rows, cols, count, tiles, cells, cells_2, times_t, image_t, sums, sums_2, copies, own_raw):
    inverse = 1.0 / jnp.sqrt(sums[:, 0:1])
    alpha_1, beta_2 = norms(sums_2)
    scale = 1.0 / (alpha_1 * beta_2)
    shift = (alpha_1 / beta_2 + beta_2 / alpha_1) * inverse
    lane = lax.broadcasted_iota(jnp.int32, (LANES, LANES), 1)
    image = jnp.zeros((LANES, LANES), jnp.float32)
    for k in range(TS):
        r, at, weight = placed(k, rows, cols, count)
        raw = scale * cells_2[pl.ds(at, 1), :] - shift * cells[pl.ds(at, 1), :]
        term = jnp.sum(tiles[k] * raw, axis=1, keepdims=True) * weight
        image = image + jnp.where(lane == r, term, 0.0)
    ray = (image_t[...] / alpha_1 - (alpha_1 * inverse) * times_t[...]) / beta_2
    own_1 = own_rows(cells)
    own_2 = scale * own_rows(cells_2) - shift * own_1
    own_raw[0] = own_1 * inverse
    own_raw[1] = own_2
    row = packed([total(own_2 * own_2), total(image * image), total(image * ray)])
    copies[...] = jnp.broadcast_to(row[None], copies.shape)


def last_kernel(rows, sums, sums_2, own_raw, update, ratio):
    beta_1 = jnp.sqrt(sums[:, 0:1])
    alpha_1, beta_2 = norms(sums_2)
    row = jnp.sum(rows[...], axis=0)
    alpha_2, beta_3 = norms(row)
    direction = own_raw[0] / alpha_1
    rho_1 = jnp.sqrt(alpha_1 * alpha_1 + beta_2 * beta_2)
    cosine, sine = alpha_1 / rho_1, beta_2 / rho_1
    found = (cosine * beta_1 / rho_1) * direction
    phi_bar = sine * beta_1
    rho_bar = -cosine * alpha_2
    direction = own_raw[1] / alpha_2 - (sine * alpha_2 / rho_1) * direction
    rho_2 = jnp.sqrt(rho_bar * rho_bar + beta_3 * beta_3)
    cosine, sine = rho_bar / rho_2, beta_3 / rho_2
    update[...] = found + (cosine * phi_bar / rho_2) * direction
    ratio[...] = sine * phi_bar / beta_1


def line_kernel(parts, copies):
    part = parts[0]
    for s in range(1, SLOTS):
        part = part + parts[s]
    for s in range(NY * NH):
        copies[s] = part


def plane_kernel(parts, copies, sums):
    y, _, _ = coordinates()
    bands = []
    for d in range(3):
        acc = jnp.zeros((JB, LANES), jnp.float32)
        for e in range(3):
            other = y + (d + e - 2)
            inside = jnp.logical_and(other >= 0, other < NY)
            other = jnp.clip(other, 0, NY - 1)
            rel = (2 - e) * JB
            term = parts[other, rel : rel + JB, :] + parts[other + NY, rel : rel + JB, :]
            acc = acc + jnp.where(inside, term, 0.0)
        bands.append(acc)
    row = parts[0, SLOT : SLOT + 1, :]
    for s in range(1, NY * NH):
        row = row + parts[s, SLOT : SLOT + 1, :]
    sums[...] = row
    block = jnp.concatenate(bands + [jnp.zeros((DEPTH - SLOT, LANES), jnp.float32)], axis=0)
    for s in range(SLOTS):
        copies[s] = block


def exchange(table):
    _, _, core = coordinates()
    pair = lax.all_gather(table.reshape(NC, SLOTS, DEPTH, LANES), "all", axis=0, axis_index_groups=PAIRS)
    half = lax.dynamic_index_in_dim(pair, core, axis=1, keepdims=False).sum(0)
    copies = call(line_kernel, shape(NY * NH, DEPTH, LANES), [VM], (swap(half, LINES),))
    copies, sums = call(
        plane_kernel, [shape(SLOTS, DEPTH, LANES), shape(1, LANES)], [VM], (swap(copies, PLANES),)
    )
    full = lax.all_gather(swap(copies, LINES), "all", axis=0, axis_index_groups=PAIRS)
    return full.reshape(TABLE, LANES), sums


def local(sensitivity, tile_rows, tile_cols, tile_count, travel_times):
    tiles = sensitivity[0]
    lists = (tile_rows, tile_cols, tile_count)
    square = shape(LANES, LANES)
    columns = pltpu.VMEM((RB, LANES, LANES), jnp.float32)
    far = pl.BlockSpec(memory_space=pl.ANY)

    table, times_t = call(
        first_kernel,
        [shape(TABLE, LANES), square],
        [SM] * 3 + [far, VM],
        (*lists, tiles, travel_times),
        [columns, columns, pltpu.SemaphoreType.DMA],
    )
    cells, sums = exchange(table)
    table, image_t = call(
        second_kernel,
        [shape(TABLE, LANES), square],
        [SM] * 3 + [VM] * 4,
        (*lists, tiles, cells, times_t, sums),
        [columns],
    )
    cells_2, sums_2 = exchange(table)
    copies, own_raw = call(
        third_kernel,
        [shape(NZ * NC, 1, LANES), shape(2, 2, LANES)],
        [SM] * 3 + [VM] * 7,
        (*lists, tiles, cells, cells_2, times_t, image_t, sums, sums_2),
    )
    rows = swap(copies, CHIPS_Z).sum(0)
    rows = swap(jnp.broadcast_to(rows[None], (NY * NX, 1, LANES)), ALL_YX)
    update, ratio = call(last_kernel, [shape(2, LANES), shape(1, 1)], [VM] * 4, (rows, sums, sums_2, own_raw))
    return update, ratio.reshape(1)


def solution(mesh):
    flat = Mesh(mesh.devices.reshape(-1), ("all",))
    every = P("all")
    return jax.shard_map(
        local, mesh=flat, in_specs=(every,) * 5, out_specs=(every, P()), check_vma=False
    )
```

time: 167 us -> 158 us (0.946)
  blocking collectives: 156 us -> 149 us
    all_to_all x8, blocking collectives: 129 us -> 123 us  [swap(): lax.all_to_all(array, 'all', 0, 0, tiled=True, axis_index_groups=groups)]
where the time goes in v3:
time: 158 us; the launch traced here: 157 us
  blocking collectives  149 us (94%)
  Pallas kernels  5.11 us (3%)
  local copies, waits for them, and re-layouts  1.9 us (1%)
    all_to_all x8, blocking collectives, swap(): lax.all_to_all(array, 'all', 0, 0, tiled=True, axis_index_groups=groups)  123 us
    all_gather x2, blocking collectives, exchange(): lax.all_gather(table.reshape(NC, SLOTS, DEPTH, LANES), 'all', axis=0, axi...  14.9 us
    all_gather x2, blocking collectives, exchange(): lax.all_gather(swap(copies, LINES), 'all', axis=0, axis_index_groups=PAIRS)  11 us
    pallas_call x8, Pallas kernels, call(): pl.pallas_call(kernel, out_shape=outs, in_specs=ins, out_specs=jax.tree.m...  5.11 us

profile of v3, /device:TPU:1, one launch (start us, length us, event | category | flops | bytes accessed | tf_op | source)
XLA Modules:
  0.0 157.1 jit_solution(14126187316827987288)
XLA Ops:
  0.7 0.0 copy-start.2
  1.3 0.0 copy-start.3
  1.3 0.0 copy-start.4
  1.4 0.0 copy-done.2
  1.4 0.6 copy-done.3
  2.0 0.0 copy-done.4
  2.0 1.2 copy-done
  3.2 1.4 shard_map.68
  4.6 12.5 %all_gather.18 = f32[2,2,24,16,128]{4,3,2,1,0:T(8,128)S(1)} all-gather(f32[1,2,24,16,128]{4,3,2,1,0:T(8,128)S(1)} %bitcast.12), channel_id=1, replica_groups={{0,1},{2,3},{4,5},{6,7},{8,9},{10,11},{12,13},{14,15},{16,17},{18,19},{..., dimensions={0}, use_global_device_ids=true | all-gather | bytes 1179648 | tf_op jit(solution)/shard_map/all_gather | solution.py:220
  17.2 0.0 copy-start.1
  17.2 19.2 %all_to_all.40.parts = f32[24,16,128]{2,1,0:T(8,128)S(1)} all-to-all(f32[24,16,128]{2,1,0:T(8,128)S(1)} %dynamic-slice_reduce_fusion.1), channel_id=1, replica_groups={{0,2,4,6,8,10,12,14,16,18,20,22,24,26,28,30,32,34,36,38,40,42,44,46},{1..., dimensions={0} | all-to-all | bytes 393216 | tf_op jit(solution)/shard_map/all_to_all | solution.py:71
  36.4 16.9 %all_to_all.41.parts = f32[16,16,128]{2,1,0:T(8,128)S(1)} all-to-all(f32[16,16,128]{2,1,0:T(8,128)S(1)} %shard_map.69), channel_id=1, replica_groups={{0,96,192,288,384,480,576,672,72,168,264,360,456,552,648,744},{1,97,193..., dimensions={0} | all-to-all | bytes 262144 | tf_op jit(solution)/shard_map/all_to_all | solution.py:71
  53.4 16.8 %all_to_all.42 = f32[24,16,128]{2,1,0:T(8,128)S(1)} all-to-all(f32[24,16,128]{2,1,0:T(8,128)S(1)} %get-tuple-element.15), channel_id=1, replica_groups={{0,2,4,6,8,10,12,14,16,18,20,22,24,26,28,30,32,34,36,38,40,42,44,46},{1..., dimensions={0} | all-to-all | bytes 393216 | tf_op jit(solution)/shard_map/all_to_all | solution.py:71
  70.2 5.5 %all-gather = f32[48,16,128]{2,1,0:T(8,128)S(1)} all-gather(f32[24,16,128]{2,1,0:T(8,128)S(1)} %all_to_all.42), channel_id=2, replica_groups={{0,1},{2,3},{4,5},{6,7},{8,9},{10,11},{12,13},{14,15},{16,17},{18,19},{..., dimensions={0}, use_global_device_ids=true | all-gather | bytes 589824 | tf_op jit(solution)/shard_map/all_gather | solution.py:226
  75.7 1.3 shard_map.71
  77.0 2.4 %all_gather.21 = f32[2,2,24,16,128]{4,3,2,1,0:T(8,128)S(1)} all-gather(f32[1,2,24,16,128]{4,3,2,1,0:T(8,128)S(1)} %bitcast.13), channel_id=1, replica_groups={{0,1},{2,3},{4,5},{6,7},{8,9},{10,11},{12,13},{14,15},{16,17},{18,19},{..., dimensions={0}, use_global_device_ids=true | all-gather | bytes 1179648 | tf_op jit(solution)/shard_map/all_gather | solution.py:220
  79.4 16.0 %all_to_all.43.parts = f32[24,16,128]{2,1,0:T(8,128)S(1)} all-to-all(f32[24,16,128]{2,1,0:T(8,128)S(1)} %dynamic-slice_reduce_fusion), channel_id=1, replica_groups={{0,2,4,6,8,10,12,14,16,18,20,22,24,26,28,30,32,34,36,38,40,42,44,46},{1..., dimensions={0} | all-to-all | bytes 393216 | tf_op jit(solution)/shard_map/all_to_all | solution.py:71
  95.4 11.6 %all_to_all.44.parts = f32[16,16,128]{2,1,0:T(8,128)S(1)} all-to-all(f32[16,16,128]{2,1,0:T(8,128)S(1)} %shard_map.72), channel_id=1, replica_groups={{0,96,192,288,384,480,576,672,72,168,264,360,456,552,648,744},{1,97,193..., dimensions={0} | all-to-all | bytes 262144 | tf_op jit(solution)/shard_map/all_to_all | solution.py:71
  107.1 16.8 %all_to_all.45 = f32[24,16,128]{2,1,0:T(8,128)S(1)} all-to-all(f32[24,16,128]{2,1,0:T(8,128)S(1)} %get-tuple-element.19), channel_id=1, replica_groups={{0,2,4,6,8,10,12,14,16,18,20,22,24,26,28,30,32,34,36,38,40,42,44,46},{1..., dimensions={0} | all-to-all | bytes 393216 | tf_op jit(solution)/shard_map/all_to_all | solution.py:71
  123.9 5.5 %all-gather.1 = f32[48,16,128]{2,1,0:T(8,128)S(1)} all-gather(f32[24,16,128]{2,1,0:T(8,128)S(1)} %all_to_all.45), channel_id=3, replica_groups={{0,1},{2,3},{4,5},{6,7},{8,9},{10,11},{12,13},{14,15},{16,17},{18,19},{..., dimensions={0}, use_global_device_ids=true | all-gather | bytes 589824 | tf_op jit(solution)/shard_map/all_gather | solution.py:226
  129.4 1.3 shard_map.74
  130.7 13.6 %all_to_all.46 = f32[24,1,128]{2,1,0:T(1,128)S(1)} all-to-all(f32[24,1,128]{2,1,0:T(1,128)S(1)} %get-tuple-element.22), channel_id=1, replica_groups={{0,1,2,3,4,5,6,7,8,9,10,11,12,13,14,15,16,17,18,19,20,21,22,23},{24,25,..., dimensions={0} | all-to-all | bytes 24576 | tf_op jit(solution)/shard_map/all_to_all | solution.py:71
  144.3 11.9 %all_to_all.47.rows = f32[32,1,128]{2,1,0:T(1,128)S(1)} all-to-all(f32[32,1,128]{2,1,0:T(1,128)S(1)} %broadcast_in_dim.2), channel_id=1, replica_groups={{0,24,48,72,96,120,144,168,192,216,240,264,288,312,336,360,384,408,432,..., dimensions={0} | all-to-all | bytes 32768 | tf_op jit(solution)/shard_map/all_to_all | solution.py:71
  156.2 0.9 shard_map.75
  (10 shorter events, 0.3 us)
Async XLA Ops:
  0.7 0.7 copy-start.2
  1.3 0.7 copy-start.3
  1.3 0.7 copy-start.4
  2.0 1.2 copy-start
  17.2 58.5 %copy-start.1 = (f32[1,16,128,128]{3,2,1,0:T(8,128)S(1)}, f32[1,16,128,128]{3,2,1,0:T(8,128)}, u32[]{:S(2)}) copy-start(f32[1,16,128,128]{3,2,1,0:T(8,128)} %param.5) | copy-start | bytes 3145732

commit v4 on v3

v4 whole, which is shorter than its diff:
```python
import jax
import jax.numpy as jnp
from jax import lax
from jax.experimental import pallas as pl
from jax.experimental.pallas import tpu as pltpu
from jax.sharding import Mesh, PartitionSpec as P

NY, NX, NZ, NC = 8, 4, 12, 2
NH = 2
SLAB = 192
SLOTS = NH * NZ
JB = SLAB // (NC * SLOTS)
SLOT = 3 * JB
NARROW = (3, JB)
PAIRED = (SLOT // 2 + 1, 2)
LANES = 128
TABLE = NC * SLOTS
TS = 16
RB = 16
VM = pl.BlockSpec(memory_space=pltpu.VMEM)
SM = pl.BlockSpec(memory_space=pltpu.SMEM)


def shape(*dims):
    return jax.ShapeDtypeStruct(dims, jnp.float32)


def call(kernel, outs, ins, args, scratch=()):
    return pl.pallas_call(
        kernel,
        out_shape=outs,
        in_specs=ins,
        out_specs=jax.tree.map(lambda _: VM, outs),
        scratch_shapes=scratch,
        compiler_params=pltpu.CompilerParams(vmem_limit_bytes=32 * 1024 * 1024),
    )(*args)


def over_slab(value):
    return (value * 43691) >> 23


def coordinates():
    me = lax.axis_index("all")
    y = over_slab(2 * me)
    rest = me - y * (NX * NZ * NC)
    return y, rest >> 1, rest & 1


def device(y, x, z, c):
    return ((y * NX + x) * NZ + z) * NC + c


PAIRS = [[device(y, x, z, 0), device(y, x, z, 1)] for y in range(NY) for x in range(NX) for z in range(NZ)]
LINES = [
    [device(y, x, z, c) for x in pair for z in range(NZ)]
    for y in range(NY)
    for pair in ((0, 1), (3, 2))
    for c in range(NC)
]
PLANES = [
    [device(y, x, z, c) for x in pair for y in range(NY)]
    for z in range(NZ)
    for pair in ((0, 3), (1, 2))
    for c in range(NC)
]
CHIPS_Z = [
    [device(y, x, z, c) for z in range(NZ) for c in range(NC)] for y in range(NY) for x in range(NX)
]
ALL_YX = [
    [device(y, x, z, c) for y in range(NY) for x in range(NX)] for z in range(NZ) for c in range(NC)
]


def swap(array, groups):
    return lax.all_to_all(array, "all", 0, 0, tiled=True, axis_index_groups=groups)


def placed(lists):
    rows, cols, count = lists
    y, _, _ = coordinates()
    places = []
    for k in range(TS):
        column = cols[0, k]
        region = over_slab(column)
        within = column - region * SLAB
        slot = jnp.clip(within >> 2, 0, TABLE - 1)
        at = jnp.clip(region - y + 1, 0, 2) * JB + (within & 3)
        weight = jnp.where(k < count[0, 0], jnp.float32(1.0), jnp.float32(0.0))
        places.append((jnp.clip(rows[0, k], 0, RB - 1), slot, at, weight))
    return places


def picked(cells, slot, at):
    return cells[slot, at >> 2, pl.ds(at & 3, 1), :]


def own_rows(cells):
    _, slot, core = coordinates()
    return cells[slot, 1, pl.ds(core * 2, 2), :]


def total(value):
    return jnp.sum(jnp.sum(value, axis=0, keepdims=True), axis=1, keepdims=True)


def packed(values):
    lane = lax.broadcasted_iota(jnp.int32, (1, LANES), 1)
    row = jnp.zeros((1, LANES), jnp.float32)
    for i, value in enumerate(values):
        row = jnp.where(lane == i, value, row)
    return row


def backward_terms(places, tiles, columns, table):
    shift = 2 if table.shape[2] == JB else 1
    for k, (r, slot, at, weight) in enumerate(places):
        term = jnp.sum(tiles[k] * columns[r], axis=0, keepdims=True) * weight
        row = pl.ds(at & (table.shape[2] - 1), 1)
        table[slot, at >> shift, row, :] = table[slot, at >> shift, row, :] + term


def first_kernel(rows, cols, count, tiles, times, table, times_t, columns):
    padded = jnp.concatenate([times[...], jnp.zeros((LANES - RB, LANES), jnp.float32)], axis=0)
    turned = padded.T
    times_t[...] = turned
    for r in range(RB):
        columns[r] = jnp.broadcast_to(turned[:, r : r + 1], (LANES, LANES))
    table[...] = jnp.zeros_like(table)
    backward_terms(placed((rows, cols, count)), tiles, columns, table)


def second_kernel(rows, cols, count, tiles, cells, times_t, table, image_t, columns):
    places = placed((rows, cols, count))
    columns[...] = jnp.zeros_like(columns)
    table[...] = jnp.zeros_like(table)
    for k, (r, slot, at, weight) in enumerate(places):
        term = jnp.sum(tiles[k] * picked(cells, slot, at), axis=1, keepdims=True) * weight
        columns[r] = columns[r] + term
    lane = lax.broadcasted_iota(jnp.int32, (LANES, LANES), 1)
    image = jnp.zeros((LANES, LANES), jnp.float32)
    for r in range(RB):
        image = jnp.where(lane == r, columns[r], image)
    image_t[...] = image
    times = times_t[...]
    own = own_rows(cells)
    row = packed([total(times * times), total(own * own), total(image * image), total(image * times)])
    row = jnp.broadcast_to(row, (2, LANES))
    for s in range(TABLE):
        table[s, SLOT // 2] = row
    backward_terms(places, tiles, columns, table)


def third_kernel(rows, cols, count, tiles, cells, cells_2, times_t, image_t, sums, copies, held):
    times_sum, cells_sum, image_sum, cross = (sums[:, i : i + 1] for i in range(4))
    beta_1 = jnp.sqrt(times_sum)
    square = cells_sum / times_sum
    alpha_1 = jnp.sqrt(square)
    beta_2 = jnp.sqrt(image_sum / cells_sum - 2.0 * (cross / times_sum) + square)
    scale = 1.0 / (beta_1 * alpha_1 * beta_2)
    shift = (alpha_1 / beta_2 + beta_2 / alpha_1) / beta_1
    lane = lax.broadcasted_iota(jnp.int32, (LANES, LANES), 1)
    image = jnp.zeros((LANES, LANES), jnp.float32)
    for k, (r, slot, at, weight) in enumerate(placed((rows, cols, count))):
        raw = scale * picked(cells_2, slot, at) - shift * picked(cells, slot, at)
        term = jnp.sum(tiles[k] * raw, axis=1, keepdims=True) * weight
        image = image + jnp.where(lane == r, term, 0.0)
    ray = (image_t[...] / (alpha_1 * beta_1) - (alpha_1 / beta_1) * times_t[...]) / beta_2
    own_1 = own_rows(cells)
    own_2 = scale * own_rows(cells_2) - shift * own_1
    row = packed([total(own_2 * own_2), total(image * image), total(image * ray)])
    copies[...] = jnp.broadcast_to(row[None], copies.shape)
    rho_1 = jnp.sqrt(alpha_1 * alpha_1 + beta_2 * beta_2)
    cosine, sine = alpha_1 / rho_1, beta_2 / rho_1
    direction = own_1 / (beta_1 * alpha_1)
    held[0] = own_2
    held[1] = (cosine * beta_1 / rho_1) * direction
    held[2] = (sine / rho_1) * direction
    for i, value in enumerate([cosine, sine, sine * beta_1]):
        held[3 + i] = jnp.broadcast_to(value, (2, LANES))


def last_kernel(rows, held, update, ratio):
    cells_sum, image_sum, cross = (jnp.sum(rows[:, :, i : i + 1], axis=0) for i in range(3))
    alpha_2 = jnp.sqrt(cells_sum)
    beta_3 = jnp.sqrt(image_sum / cells_sum - 2.0 * cross + cells_sum)
    direction = held[0] / alpha_2 - alpha_2 * held[2]
    rho_bar = -held[3] * alpha_2
    rho_2 = jnp.sqrt(rho_bar * rho_bar + beta_3 * beta_3)
    update[...] = held[1] + (rho_bar / rho_2 * held[5] / rho_2) * direction
    ratio[...] = (beta_3 / rho_2[0:1, 0:1]) * held[4][0:1, 0:1]


def line_kernel(parts, copies):
    part = parts[0]
    for s in range(1, SLOTS):
        part = part + parts[s]
    for s in range(NY * NH):
        copies[s] = part


def plane_kernel(parts, copies, *sums):
    y, _, _ = coordinates()
    width = parts.shape[2]
    for d in range(3):
        for i in range(JB // width):
            acc = jnp.zeros((width, LANES), jnp.float32)
            for e in range(3):
                other = y + (d + e - 2)
                inside = jnp.logical_and(other >= 0, other < NY)
                other = jnp.clip(other, 0, NY - 1)
                at = (2 - e) * (JB // width) + i
                acc = acc + jnp.where(inside, parts[other, at] + parts[other + NY, at], 0.0)
            for s in range(SLOTS):
                copies[s, d, i * width : (i + 1) * width, :] = acc
    if sums:
        row = parts[0, SLOT // 2]
        for s in range(1, NY * NH):
            row = row + parts[s, SLOT // 2]
        sums[0][...] = row[0:1, :]


def exchange(table):
    _, _, core = coordinates()
    slot = table.shape[1:]
    pair = lax.all_gather(table.reshape((NC, SLOTS) + slot), "all", axis=0, axis_index_groups=PAIRS)
    half = lax.dynamic_index_in_dim(pair, core, axis=1, keepdims=False).sum(0)
    copies = call(line_kernel, shape(NY * NH, *slot), [VM], (swap(half, LINES),))
    outs = [shape(SLOTS, *NARROW, LANES)] + [shape(1, LANES)] * (slot[1] != JB)
    copies, *sums = call(plane_kernel, outs, [VM], (swap(copies, PLANES),))
    full = lax.all_gather(swap(copies, LINES), "all", axis=0, axis_index_groups=PAIRS)
    return full.reshape(TABLE, *NARROW, LANES), *sums


def local(sensitivity, tile_rows, tile_cols, tile_count, travel_times):
    tiles = sensitivity[0]
    lists = (tile_rows, tile_cols, tile_count.reshape(1, 1))
    square = shape(LANES, LANES)
    columns = pltpu.VMEM((RB, LANES, LANES), jnp.float32)

    table, times_t = call(
        first_kernel,
        [shape(TABLE, *NARROW, LANES), square],
        [SM] * 3 + [VM] * 2,
        (*lists, tiles, travel_times),
        [columns],
    )
    (cells,) = exchange(table)
    table, image_t = call(
        second_kernel,
        [shape(TABLE, *PAIRED, LANES), square],
        [SM] * 3 + [VM] * 3,
        (*lists, tiles, cells, times_t),
        [columns],
    )
    cells_2, sums = exchange(table)
    copies, held = call(
        third_kernel,
        [shape(NZ * NC, 1, LANES), shape(6, 2, LANES)],
        [SM] * 3 + [VM] * 6,
        (*lists, tiles, cells, cells_2, times_t, image_t, sums),
    )
    rows = swap(copies, CHIPS_Z).sum(0)
    rows = swap(jnp.broadcast_to(rows[None], (NY * NX, 1, LANES)), ALL_YX)
    update, ratio = call(last_kernel, [shape(2, LANES), shape(1, 1)], [VM] * 2, (rows, held))
    return update, ratio.reshape(1)


def solution(mesh):
    flat = Mesh(mesh.devices.reshape(-1), ("all",))
    every = P("all")
    return jax.shard_map(
        local, mesh=flat, in_specs=(every,) * 5, out_specs=(every, P()), check_vma=False
    )
```

time: 158 us -> 152 us (0.962)
  blocking collectives: 149 us -> 144 us
    all_to_all x8, blocking collectives: 123 us -> 118 us  [swap(): lax.all_to_all(array, 'all', 0, 0, tiled=True, axis_index_groups=groups)]
where the time goes in v4:
time: 152 us
  blocking collectives  144 us (95%)
  Pallas kernels  4.81 us (3%)
  local copies, waits for them, and re-layouts  2.08 us (1%)
    all_to_all x8, blocking collectives, swap(): lax.all_to_all(array, 'all', 0, 0, tiled=True, axis_index_groups=groups)  118 us
    all_gather x2, blocking collectives, exchange(): lax.all_gather(table.reshape((NC, SLOTS) + slot), 'all', axis=0, axis_ind...  14.7 us
    all_gather x2, blocking collectives, exchange(): lax.all_gather(swap(copies, LINES), 'all', axis=0, axis_index_groups=PAIRS)  11 us
    pallas_call x8, Pallas kernels, call(): pl.pallas_call(kernel, out_shape=outs, in_specs=ins, out_specs=jax.tree.m...  4.81 us

profile of v4, /device:TPU:1, one launch (start us, length us, event | category | flops | bytes accessed | tf_op | source)
XLA Modules:
  0.0 151.9 jit_solution(10774940971599222966)
XLA Ops:
  1.3 0.0 copy-done.2
  1.3 0.6 copy-done.3
  2.0 0.0 copy-done.4
  2.0 1.2 copy-done
  3.2 1.2 shard_map.68
  4.4 12.4 %all_gather.18 = f32[2,2,24,3,4,128]{5,2,4,3,1,0:T(8,128)S(1)} all-gather(f32[1,2,24,3,4,128]{5,2,4,3,1,0:T(8,128)S(1)} %copy.9), channel_id=1, replica_groups={{0,1},{2,3},{4,5},{6,7},{8,9},{10,11},{12,13},{14,15},{16,17},{18,19},{..., dimensions={0}, use_global_device_ids=true | all-gather | bytes 884736 | tf_op jit(solution)/shard_map/all_gather | solution.py:226
  16.8 0.0 copy-start.1
  16.9 18.2 %all_to_all.40.parts = f32[24,3,4,128]{3,2,1,0:T(4,128)S(1)} all-to-all(f32[24,3,4,128]{3,2,1,0:T(4,128)S(1)} %copy.10), channel_id=1, replica_groups={{0,2,4,6,8,10,12,14,16,18,20,22,24,26,28,30,32,34,36,38,40,42,44,46},{1..., dimensions={0} | all-to-all | bytes 294912 | tf_op jit(solution)/shard_map/all_to_all | solution.py:76
  35.1 16.9 %all_to_all.41.parts = f32[16,3,4,128]{3,2,1,0:T(4,128)S(1)} all-to-all(f32[16,3,4,128]{3,2,1,0:T(4,128)S(1)} %shard_map.69), channel_id=1, replica_groups={{0,96,192,288,384,480,576,672,72,168,264,360,456,552,648,744},{1,97,193..., dimensions={0} | all-to-all | bytes 196608 | tf_op jit(solution)/shard_map/all_to_all | solution.py:76
  52.0 15.5 %all_to_all.42 = f32[24,3,4,128]{3,2,1,0:T(4,128)S(1)} all-to-all(f32[24,3,4,128]{3,2,1,0:T(4,128)S(1)} %shard_map.70), channel_id=1, replica_groups={{0,2,4,6,8,10,12,14,16,18,20,22,24,26,28,30,32,34,36,38,40,42,44,46},{1..., dimensions={0} | all-to-all | bytes 294912 | tf_op jit(solution)/shard_map/all_to_all | solution.py:76
  67.5 5.6 %all-gather.cells = f32[48,3,4,128]{3,2,1,0:T(4,128)S(1)} all-gather(f32[24,3,4,128]{3,2,1,0:T(4,128)S(1)} %all_to_all.42), channel_id=2, replica_groups={{0,1},{2,3},{4,5},{6,7},{8,9},{10,11},{12,13},{14,15},{16,17},{18,19},{..., dimensions={0}, use_global_device_ids=true | all-gather | bytes 442368 | tf_op jit(solution)/shard_map/all_gather | solution.py:231
  73.1 1.3 shard_map.71
  74.5 2.3 %all_gather.21 = f32[2,2,24,7,2,128]{5,2,4,3,1,0:T(8,128)S(1)} all-gather(f32[1,2,24,7,2,128]{5,2,4,3,1,0:T(8,128)S(1)} %copy.11), channel_id=1, replica_groups={{0,1},{2,3},{4,5},{6,7},{8,9},{10,11},{12,13},{14,15},{16,17},{18,19},{..., dimensions={0}, use_global_device_ids=true | all-gather | bytes 1032192 | tf_op jit(solution)/shard_map/all_gather | solution.py:226
  76.8 0.1 copy.12
  76.9 15.3 %all_to_all.43.parts = f32[24,7,2,128]{3,2,1,0:T(2,128)S(1)} all-to-all(f32[24,7,2,128]{3,2,1,0:T(2,128)S(1)} %copy.12), channel_id=1, replica_groups={{0,2,4,6,8,10,12,14,16,18,20,22,24,26,28,30,32,34,36,38,40,42,44,46},{1..., dimensions={0} | all-to-all | bytes 344064 | tf_op jit(solution)/shard_map/all_to_all | solution.py:76
  92.1 0.1 shard_map.72
  92.2 11.2 %all_to_all.44.parts = f32[16,7,2,128]{3,2,1,0:T(2,128)S(1)} all-to-all(f32[16,7,2,128]{3,2,1,0:T(2,128)S(1)} %shard_map.72), channel_id=1, replica_groups={{0,96,192,288,384,480,576,672,72,168,264,360,456,552,648,744},{1,97,193..., dimensions={0} | all-to-all | bytes 229376 | tf_op jit(solution)/shard_map/all_to_all | solution.py:76
  103.4 0.1 shard_map.73
  103.5 16.0 %all_to_all.45 = f32[24,3,4,128]{3,2,1,0:T(4,128)S(1)} all-to-all(f32[24,3,4,128]{3,2,1,0:T(4,128)S(1)} %get-tuple-element.15), channel_id=1, replica_groups={{0,2,4,6,8,10,12,14,16,18,20,22,24,26,28,30,32,34,36,38,40,42,44,46},{1..., dimensions={0} | all-to-all | bytes 294912 | tf_op jit(solution)/shard_map/all_to_all | solution.py:76
  119.5 5.4 %all-gather.1.cells_2 = f32[48,3,4,128]{3,2,1,0:T(4,128)S(1)} all-gather(f32[24,3,4,128]{3,2,1,0:T(4,128)S(1)} %all_to_all.45), channel_id=3, replica_groups={{0,1},{2,3},{4,5},{6,7},{8,9},{10,11},{12,13},{14,15},{16,17},{18,19},{..., dimensions={0}, use_global_device_ids=true | all-gather | bytes 442368 | tf_op jit(solution)/shard_map/all_gather | solution.py:231
  124.9 1.3 shard_map.74
  126.2 13.3 %all_to_all.46 = f32[24,1,128]{2,1,0:T(1,128)S(1)} all-to-all(f32[24,1,128]{2,1,0:T(1,128)S(1)} %get-tuple-element.18), channel_id=1, replica_groups={{0,1,2,3,4,5,6,7,8,9,10,11,12,13,14,15,16,17,18,19,20,21,22,23},{24,25,..., dimensions={0} | all-to-all | bytes 24576 | tf_op jit(solution)/shard_map/all_to_all | solution.py:76
  139.5 11.5 %all_to_all.47.rows = f32[32,1,128]{2,1,0:T(1,128)S(1)} all-to-all(f32[32,1,128]{2,1,0:T(1,128)S(1)} %broadcast_in_dim.2), channel_id=1, replica_groups={{0,24,48,72,96,120,144,168,192,216,240,264,288,312,336,360,384,408,432,..., dimensions={0} | all-to-all | bytes 32768 | tf_op jit(solution)/shard_map/all_to_all | solution.py:76
  151.0 0.9 shard_map.75
  (14 shorter events, 0.3 us)
Async XLA Ops:
  0.6 0.7 copy-start.2
  1.3 0.7 copy-start.3
  1.3 0.7 copy-start.4
  2.0 1.2 copy-start
  16.8 56.3 %copy-start.1 = (f32[1,16,128,128]{3,2,1,0:T(8,128)S(1)}, f32[1,16,128,128]{3,2,1,0:T(8,128)}, u32[]{:S(2)}) copy-start(f32[1,16,128,128]{3,2,1,0:T(8,128)} %param.5) | copy-start | bytes 3145732

commit v5 on v4

--- a/solution.py
+++ b/solution.py
@@ -25,14 +25,14 @@
     return jax.ShapeDtypeStruct(dims, jnp.float32)
 
 
-def call(kernel, outs, ins, args, scratch=()):
+def call(kernel, outs, ins, args, scratch=(), room=32 * 1024):
     return pl.pallas_call(
         kernel,
         out_shape=outs,
         in_specs=ins,
         out_specs=jax.tree.map(lambda _: VM, outs),
         scratch_shapes=scratch,
-        compiler_params=pltpu.CompilerParams(vmem_limit_bytes=32 * 1024 * 1024),
+        compiler_params=pltpu.CompilerParams(vmem_limit_bytes=room * 1024),
     )(*args)
 
 
@@ -86,7 +86,7 @@
         within = column - region * SLAB
         slot = jnp.clip(within >> 2, 0, TABLE - 1)
         at = jnp.clip(region - y + 1, 0, 2) * JB + (within & 3)
-        weight = jnp.where(k < count[0, 0], jnp.float32(1.0), jnp.float32(0.0))
+        weight = jnp.where(k < count[0], jnp.float32(1.0), jnp.float32(0.0))
         places.append((jnp.clip(rows[0, k], 0, RB - 1), slot, at, weight))
     return places
 
@@ -120,20 +120,35 @@
         table[slot, at >> shift, row, :] = table[slot, at >> shift, row, :] + term
 
 
-def first_kernel(rows, cols, count, tiles, times, table, times_t, columns):
+def started(pairs, sems):
+    moves = [pltpu.make_async_copy(src, dst, sems.at[i]) for i, (src, dst) in enumerate(pairs)]
+    for move in moves:
+        move.start()
+    return moves
+
+
+def first_kernel(rows_far, cols_far, count, tiles_far, times, table, times_t, columns, tiles, rows, cols, sems):
+    moves = started([(tiles_far, tiles), (rows_far, rows), (cols_far, cols)], sems)
     padded = jnp.concatenate([times[...], jnp.zeros((LANES - RB, LANES), jnp.float32)], axis=0)
     turned = padded.T
     times_t[...] = turned
     for r in range(RB):
         columns[r] = jnp.broadcast_to(turned[:, r : r + 1], (LANES, LANES))
     table[...] = jnp.zeros_like(table)
-    backward_terms(placed((rows, cols, count)), tiles, columns, table)
-
-
-def second_kernel(rows, cols, count, tiles, cells, times_t, table, image_t, columns):
+    moves[1].wait()
+    moves[2].wait()
     places = placed((rows, cols, count))
+    moves[0].wait()
+    backward_terms(places, tiles, columns, table)
+
+
+def second_kernel(rows_far, cols_far, count, tiles, cells, times_t, table, image_t, columns, rows, cols, sems):
+    moves = started([(rows_far, rows), (cols_far, cols)], sems)
     columns[...] = jnp.zeros_like(columns)
     table[...] = jnp.zeros_like(table)
+    moves[0].wait()
+    moves[1].wait()
+    places = placed((rows, cols, count))
     for k, (r, slot, at, weight) in enumerate(places):
         term = jnp.sum(tiles[k] * picked(cells, slot, at), axis=1, keepdims=True) * weight
         columns[r] = columns[r] + term
@@ -160,11 +175,11 @@
     scale = 1.0 / (beta_1 * alpha_1 * beta_2)
     shift = (alpha_1 / beta_2 + beta_2 / alpha_1) / beta_1
     lane = lax.broadcasted_iota(jnp.int32, (LANES, LANES), 1)
-    image = jnp.zeros((LANES, LANES), jnp.float32)
+    image_2 = jnp.zeros((LANES, LANES), jnp.float32)
     for k, (r, slot, at, weight) in enumerate(placed((rows, cols, count))):
-        raw = scale * picked(cells_2, slot, at) - shift * picked(cells, slot, at)
-        term = jnp.sum(tiles[k] * raw, axis=1, keepdims=True) * weight
-        image = image + jnp.where(lane == r, term, 0.0)
+        term = jnp.sum(tiles[k] * picked(cells_2, slot, at), axis=1, keepdims=True) * weight
+        image_2 = image_2 + jnp.where(lane == r, term, 0.0)
+    image = scale * image_2 - shift * image_t[...]
     ray = (image_t[...] / (alpha_1 * beta_1) - (alpha_1 / beta_1) * times_t[...]) / beta_2
     own_1 = own_rows(cells)
     own_2 = scale * own_rows(cells_2) - shift * own_1
@@ -234,24 +249,27 @@
 
 def local(sensitivity, tile_rows, tile_cols, tile_count, travel_times):
     tiles = sensitivity[0]
-    lists = (tile_rows, tile_cols, tile_count.reshape(1, 1))
+    lists = (tile_rows, tile_cols, tile_count)
     square = shape(LANES, LANES)
     columns = pltpu.VMEM((RB, LANES, LANES), jnp.float32)
+    far = pl.BlockSpec(memory_space=pl.ANY)
+    short = [pltpu.SMEM((1, TS), jnp.int32)] * 2
 
     table, times_t = call(
         first_kernel,
         [shape(TABLE, *NARROW, LANES), square],
-        [SM] * 3 + [VM] * 2,
+        [far, far, SM, far, VM],
         (*lists, tiles, travel_times),
-        [columns],
+        [columns, columns, *short, pltpu.SemaphoreType.DMA((3,))],
+        54528,
     )
     (cells,) = exchange(table)
     table, image_t = call(
         second_kernel,
         [shape(TABLE, *PAIRED, LANES), square],
-        [SM] * 3 + [VM] * 3,
+        [far, far, SM] + [VM] * 3,
         (*lists, tiles, cells, times_t),
-        [columns],
+        [columns, *short, pltpu.SemaphoreType.DMA((2,))],
     )
     cells_2, sums = exchange(table)
     copies, held = call(

time: 152 us -> 152 us (level)
  no operation moved by 1% of the time
where the time goes in v5:
time: 152 us; the launch traced here: 151 us
  blocking collectives  144 us (95%)
  Pallas kernels  5.15 us (3%)
    all_to_all x8, blocking collectives, swap(): lax.all_to_all(array, 'all', 0, 0, tiled=True, axis_index_groups=groups)  118 us
    all_gather x2, blocking collectives, exchange(): lax.all_gather(table.reshape((NC, SLOTS) + slot), 'all', axis=0, axis_ind...  14.7 us
    all_gather x2, blocking collectives, exchange(): lax.all_gather(swap(copies, LINES), 'all', axis=0, axis_index_groups=PAIRS)  11 us
    pallas_call x8, Pallas kernels, call(): pl.pallas_call(kernel, out_shape=outs, in_specs=ins, out_specs=jax.tree.m...  5.15 us

profile of v5, /device:TPU:1, one launch (start us, length us, event | category | flops | bytes accessed | tf_op | source)
XLA Modules:
  0.0 151.0 jit_solution(4380957355562986035)
XLA Ops:
  0.6 0.0 copy-start.1
  1.3 0.0 copy-done.1
  1.3 0.6 copy-done.2
  2.0 0.0 copy-done.3
  2.0 1.7 %shard_map.68 = (f32[48,3,4,128]{3,2,1,0:T(4,128)S(1)}, f32[128,128]{1,0:T(8,128)S(1)}) custom-call(s32[1,16]{1,0:T(1,128)S(1)} %copy-done.2, s32[1,16]{1,0:T(1,128)S(1)} %copy-done.3, s32[1]{0:T(128)S(6)} %copy.13.count, f32[16,128,128]{2,1,0:T(8,128)} %bitcast.4, f32[16,128]{1,0:T(8,128)S(1)} %copy-done.1), custom_call_target="tpu_custom_call" | custom-call | tf_op jit(solution)/shard_map/pallas_call | solution.py:29
  3.7 12.4 %all_gather.18 = f32[2,2,24,3,4,128]{5,2,4,3,1,0:T(8,128)S(1)} all-gather(f32[1,2,24,3,4,128]{5,2,4,3,1,0:T(8,128)S(1)} %copy.9), channel_id=1, replica_groups={{0,1},{2,3},{4,5},{6,7},{8,9},{10,11},{12,13},{14,15},{16,17},{18,19},{..., dimensions={0}, use_global_device_ids=true | all-gather | bytes 884736 | tf_op jit(solution)/shard_map/all_gather | solution.py:241
  16.1 0.0 copy-start
  16.1 18.2 %all_to_all.40.parts = f32[24,3,4,128]{3,2,1,0:T(4,128)S(1)} all-to-all(f32[24,3,4,128]{3,2,1,0:T(4,128)S(1)} %copy.10), channel_id=1, replica_groups={{0,2,4,6,8,10,12,14,16,18,20,22,24,26,28,30,32,34,36,38,40,42,44,46},{1..., dimensions={0} | all-to-all | bytes 294912 | tf_op jit(solution)/shard_map/all_to_all | solution.py:76
  34.3 16.9 %all_to_all.41.parts = f32[16,3,4,128]{3,2,1,0:T(4,128)S(1)} all-to-all(f32[16,3,4,128]{3,2,1,0:T(4,128)S(1)} %shard_map.69), channel_id=1, replica_groups={{0,96,192,288,384,480,576,672,72,168,264,360,456,552,648,744},{1,97,193..., dimensions={0} | all-to-all | bytes 196608 | tf_op jit(solution)/shard_map/all_to_all | solution.py:76
  51.3 15.5 %all_to_all.42 = f32[24,3,4,128]{3,2,1,0:T(4,128)S(1)} all-to-all(f32[24,3,4,128]{3,2,1,0:T(4,128)S(1)} %shard_map.70), channel_id=1, replica_groups={{0,2,4,6,8,10,12,14,16,18,20,22,24,26,28,30,32,34,36,38,40,42,44,46},{1..., dimensions={0} | all-to-all | bytes 294912 | tf_op jit(solution)/shard_map/all_to_all | solution.py:76
  66.8 5.6 %all-gather.cells = f32[48,3,4,128]{3,2,1,0:T(4,128)S(1)} all-gather(f32[24,3,4,128]{3,2,1,0:T(4,128)S(1)} %all_to_all.42), channel_id=2, replica_groups={{0,1},{2,3},{4,5},{6,7},{8,9},{10,11},{12,13},{14,15},{16,17},{18,19},{..., dimensions={0}, use_global_device_ids=true | all-gather | bytes 442368 | tf_op jit(solution)/shard_map/all_gather | solution.py:246
  72.4 1.2 shard_map.71
  73.7 2.3 %all_gather.21 = f32[2,2,24,7,2,128]{5,2,4,3,1,0:T(8,128)S(1)} all-gather(f32[1,2,24,7,2,128]{5,2,4,3,1,0:T(8,128)S(1)} %copy.11), channel_id=1, replica_groups={{0,1},{2,3},{4,5},{6,7},{8,9},{10,11},{12,13},{14,15},{16,17},{18,19},{..., dimensions={0}, use_global_device_ids=true | all-gather | bytes 1032192 | tf_op jit(solution)/shard_map/all_gather | solution.py:241
  76.0 0.1 copy.12
  76.1 15.3 %all_to_all.43.parts = f32[24,7,2,128]{3,2,1,0:T(2,128)S(1)} all-to-all(f32[24,7,2,128]{3,2,1,0:T(2,128)S(1)} %copy.12), channel_id=1, replica_groups={{0,2,4,6,8,10,12,14,16,18,20,22,24,26,28,30,32,34,36,38,40,42,44,46},{1..., dimensions={0} | all-to-all | bytes 344064 | tf_op jit(solution)/shard_map/all_to_all | solution.py:76
  91.4 0.1 shard_map.72
  91.4 11.2 %all_to_all.44.parts = f32[16,7,2,128]{3,2,1,0:T(2,128)S(1)} all-to-all(f32[16,7,2,128]{3,2,1,0:T(2,128)S(1)} %shard_map.72), channel_id=1, replica_groups={{0,96,192,288,384,480,576,672,72,168,264,360,456,552,648,744},{1,97,193..., dimensions={0} | all-to-all | bytes 229376 | tf_op jit(solution)/shard_map/all_to_all | solution.py:76
  102.7 0.1 shard_map.73
  102.7 16.0 %all_to_all.45 = f32[24,3,4,128]{3,2,1,0:T(4,128)S(1)} all-to-all(f32[24,3,4,128]{3,2,1,0:T(4,128)S(1)} %get-tuple-element.15), channel_id=1, replica_groups={{0,2,4,6,8,10,12,14,16,18,20,22,24,26,28,30,32,34,36,38,40,42,44,46},{1..., dimensions={0} | all-to-all | bytes 294912 | tf_op jit(solution)/shard_map/all_to_all | solution.py:76
  118.7 5.4 %all-gather.1.cells_2 = f32[48,3,4,128]{3,2,1,0:T(4,128)S(1)} all-gather(f32[24,3,4,128]{3,2,1,0:T(4,128)S(1)} %all_to_all.45), channel_id=3, replica_groups={{0,1},{2,3},{4,5},{6,7},{8,9},{10,11},{12,13},{14,15},{16,17},{18,19},{..., dimensions={0}, use_global_device_ids=true | all-gather | bytes 442368 | tf_op jit(solution)/shard_map/all_gather | solution.py:246
  124.1 1.2 shard_map.74
  125.3 13.2 %all_to_all.46 = f32[24,1,128]{2,1,0:T(1,128)S(1)} all-to-all(f32[24,1,128]{2,1,0:T(1,128)S(1)} %get-tuple-element.18), channel_id=1, replica_groups={{0,1,2,3,4,5,6,7,8,9,10,11,12,13,14,15,16,17,18,19,20,21,22,23},{24,25,..., dimensions={0} | all-to-all | bytes 24576 | tf_op jit(solution)/shard_map/all_to_all | solution.py:76
  138.6 11.5 %all_to_all.47.rows = f32[32,1,128]{2,1,0:T(1,128)S(1)} all-to-all(f32[32,1,128]{2,1,0:T(1,128)S(1)} %broadcast_in_dim.2), channel_id=1, replica_groups={{0,24,48,72,96,120,144,168,192,216,240,264,288,312,336,360,384,408,432,..., dimensions={0} | all-to-all | bytes 32768 | tf_op jit(solution)/shard_map/all_to_all | solution.py:76
  150.1 0.9 shard_map.75
  (12 shorter events, 0.3 us)
Async XLA Ops:
  0.6 0.7 copy-start.1
  1.3 0.7 copy-start.2
  1.3 0.7 copy-start.3
  16.1 56.3 %copy-start = (f32[1,16,128,128]{3,2,1,0:T(8,128)S(1)}, f32[1,16,128,128]{3,2,1,0:T(8,128)}, u32[]{:S(2)}) copy-start(f32[1,16,128,128]{3,2,1,0:T(8,128)} %param.5) | copy-start | bytes 3145732

commit v6 on v5

--- a/solution.py
+++ b/solution.py
@@ -53,7 +53,7 @@
 
 PAIRS = [[device(y, x, z, 0), device(y, x, z, 1)] for y in range(NY) for x in range(NX) for z in range(NZ)]
 LINES = [
-    [device(y, x, z, c) for x in pair for z in range(NZ)]
+    [device(y, x, z, c) for z in range(NZ) for x in pair]
     for y in range(NY)
     for pair in ((0, 1), (3, 2))
     for c in range(NC)

time: 152 us -> 151 us (level)
  no operation moved by 1% of the time
where the time goes in v6:
time: 151 us
  blocking collectives  143 us (95%)
  Pallas kernels  5.15 us (3%)
    all_to_all x8, blocking collectives, swap(): lax.all_to_all(array, 'all', 0, 0, tiled=True, axis_index_groups=groups)  118 us
    all_gather x2, blocking collectives, exchange(): lax.all_gather(table.reshape((NC, SLOTS) + slot), 'all', axis=0, axis_ind...  14.7 us
    all_gather x2, blocking collectives, exchange(): lax.all_gather(swap(copies, LINES), 'all', axis=0, axis_index_groups=PAIRS)  10.9 us
    pallas_call x8, Pallas kernels, call(): pl.pallas_call(kernel, out_shape=outs, in_specs=ins, out_specs=jax.tree.m...  5.15 us

profile of v6, /device:TPU:1, one launch (start us, length us, event | category | flops | bytes accessed | tf_op | source)
XLA Modules:
  0.0 150.7 jit_solution(7388787600360369127)
XLA Ops:
  0.6 0.0 copy-start.1
  1.3 0.0 copy-done.1
  1.3 0.6 copy-done.2
  2.0 0.0 copy-done.3
  2.0 1.7 %shard_map.68 = (f32[48,3,4,128]{3,2,1,0:T(4,128)S(1)}, f32[128,128]{1,0:T(8,128)S(1)}) custom-call(s32[1,16]{1,0:T(1,128)S(1)} %copy-done.2, s32[1,16]{1,0:T(1,128)S(1)} %copy-done.3, s32[1]{0:T(128)S(6)} %copy.13.count, f32[16,128,128]{2,1,0:T(8,128)} %bitcast.4, f32[16,128]{1,0:T(8,128)S(1)} %copy-done.1), custom_call_target="tpu_custom_call" | custom-call | tf_op jit(solution)/shard_map/pallas_call | solution.py:29
  3.7 12.4 %all_gather.18 = f32[2,2,24,3,4,128]{5,2,4,3,1,0:T(8,128)S(1)} all-gather(f32[1,2,24,3,4,128]{5,2,4,3,1,0:T(8,128)S(1)} %copy.9), channel_id=1, replica_groups={{0,1},{2,3},{4,5},{6,7},{8,9},{10,11},{12,13},{14,15},{16,17},{18,19},{..., dimensions={0}, use_global_device_ids=true | all-gather | bytes 884736 | tf_op jit(solution)/shard_map/all_gather | solution.py:241
  16.1 0.0 copy-start
  16.1 17.6 %all_to_all.40.parts = f32[24,3,4,128]{3,2,1,0:T(4,128)S(1)} all-to-all(f32[24,3,4,128]{3,2,1,0:T(4,128)S(1)} %copy.10), channel_id=1, replica_groups={{0,24,2,26,4,28,6,30,8,32,10,34,12,36,14,38,16,40,18,42,20,44,22,46},{1..., dimensions={0} | all-to-all | bytes 294912 | tf_op jit(solution)/shard_map/all_to_all | solution.py:76
  33.8 16.9 %all_to_all.41.parts = f32[16,3,4,128]{3,2,1,0:T(4,128)S(1)} all-to-all(f32[16,3,4,128]{3,2,1,0:T(4,128)S(1)} %shard_map.69), channel_id=1, replica_groups={{0,96,192,288,384,480,576,672,72,168,264,360,456,552,648,744},{1,97,193..., dimensions={0} | all-to-all | bytes 196608 | tf_op jit(solution)/shard_map/all_to_all | solution.py:76
  50.7 15.7 %all_to_all.42 = f32[24,3,4,128]{3,2,1,0:T(4,128)S(1)} all-to-all(f32[24,3,4,128]{3,2,1,0:T(4,128)S(1)} %shard_map.70), channel_id=1, replica_groups={{0,24,2,26,4,28,6,30,8,32,10,34,12,36,14,38,16,40,18,42,20,44,22,46},{1..., dimensions={0} | all-to-all | bytes 294912 | tf_op jit(solution)/shard_map/all_to_all | solution.py:76
  66.4 5.4 %all-gather.cells = f32[48,3,4,128]{3,2,1,0:T(4,128)S(1)} all-gather(f32[24,3,4,128]{3,2,1,0:T(4,128)S(1)} %all_to_all.42), channel_id=2, replica_groups={{0,1},{2,3},{4,5},{6,7},{8,9},{10,11},{12,13},{14,15},{16,17},{18,19},{..., dimensions={0}, use_global_device_ids=true | all-gather | bytes 442368 | tf_op jit(solution)/shard_map/all_gather | solution.py:246
  71.8 1.2 shard_map.71
  73.0 2.3 %all_gather.21 = f32[2,2,24,7,2,128]{5,2,4,3,1,0:T(8,128)S(1)} all-gather(f32[1,2,24,7,2,128]{5,2,4,3,1,0:T(8,128)S(1)} %copy.11), channel_id=1, replica_groups={{0,1},{2,3},{4,5},{6,7},{8,9},{10,11},{12,13},{14,15},{16,17},{18,19},{..., dimensions={0}, use_global_device_ids=true | all-gather | bytes 1032192 | tf_op jit(solution)/shard_map/all_gather | solution.py:241
  75.4 0.1 copy.12
  75.5 15.3 %all_to_all.43.parts = f32[24,7,2,128]{3,2,1,0:T(2,128)S(1)} all-to-all(f32[24,7,2,128]{3,2,1,0:T(2,128)S(1)} %copy.12), channel_id=1, replica_groups={{0,24,2,26,4,28,6,30,8,32,10,34,12,36,14,38,16,40,18,42,20,44,22,46},{1..., dimensions={0} | all-to-all | bytes 344064 | tf_op jit(solution)/shard_map/all_to_all | solution.py:76
  90.8 0.1 shard_map.72
  90.8 11.2 %all_to_all.44.parts = f32[16,7,2,128]{3,2,1,0:T(2,128)S(1)} all-to-all(f32[16,7,2,128]{3,2,1,0:T(2,128)S(1)} %shard_map.72), channel_id=1, replica_groups={{0,96,192,288,384,480,576,672,72,168,264,360,456,552,648,744},{1,97,193..., dimensions={0} | all-to-all | bytes 229376 | tf_op jit(solution)/shard_map/all_to_all | solution.py:76
  102.0 0.1 shard_map.73
  102.1 15.7 %all_to_all.45 = f32[24,3,4,128]{3,2,1,0:T(4,128)S(1)} all-to-all(f32[24,3,4,128]{3,2,1,0:T(4,128)S(1)} %get-tuple-element.15), channel_id=1, replica_groups={{0,24,2,26,4,28,6,30,8,32,10,34,12,36,14,38,16,40,18,42,20,44,22,46},{1..., dimensions={0} | all-to-all | bytes 294912 | tf_op jit(solution)/shard_map/all_to_all | solution.py:76
  117.7 5.5 %all-gather.1.cells_2 = f32[48,3,4,128]{3,2,1,0:T(4,128)S(1)} all-gather(f32[24,3,4,128]{3,2,1,0:T(4,128)S(1)} %all_to_all.45), channel_id=3, replica_groups={{0,1},{2,3},{4,5},{6,7},{8,9},{10,11},{12,13},{14,15},{16,17},{18,19},{..., dimensions={0}, use_global_device_ids=true | all-gather | bytes 442368 | tf_op jit(solution)/shard_map/all_gather | solution.py:246
  123.2 1.2 shard_map.74
  124.4 13.7 %all_to_all.46 = f32[24,1,128]{2,1,0:T(1,128)S(1)} all-to-all(f32[24,1,128]{2,1,0:T(1,128)S(1)} %get-tuple-element.18), channel_id=1, replica_groups={{0,1,2,3,4,5,6,7,8,9,10,11,12,13,14,15,16,17,18,19,20,21,22,23},{24,25,..., dimensions={0} | all-to-all | bytes 24576 | tf_op jit(solution)/shard_map/all_to_all | solution.py:76
  138.2 11.5 %all_to_all.47.rows = f32[32,1,128]{2,1,0:T(1,128)S(1)} all-to-all(f32[32,1,128]{2,1,0:T(1,128)S(1)} %broadcast_in_dim.2), channel_id=1, replica_groups={{0,24,48,72,96,120,144,168,192,216,240,264,288,312,336,360,384,408,432,..., dimensions={0} | all-to-all | bytes 32768 | tf_op jit(solution)/shard_map/all_to_all | solution.py:76
  149.8 0.9 shard_map.75
  (12 shorter events, 0.3 us)
Async XLA Ops:
  0.6 0.7 copy-start.1
  1.3 0.7 copy-start.2
  1.3 0.7 copy-start.3
  16.1 55.7 %copy-start = (f32[1,16,128,128]{3,2,1,0:T(8,128)S(1)}, f32[1,16,128,128]{3,2,1,0:T(8,128)}, u32[]{:S(2)}) copy-start(f32[1,16,128,128]{3,2,1,0:T(8,128)} %param.5) | copy-start | bytes 3145732

commit v7 on v6

--- a/solution.py
+++ b/solution.py
@@ -112,9 +112,10 @@
     return row
 
 
-def backward_terms(places, tiles, columns, table):
+def backward_terms(places, tiles, columns, table, first=0, end=TS):
     shift = 2 if table.shape[2] == JB else 1
-    for k, (r, slot, at, weight) in enumerate(places):
+    for k in range(first, end):
+        r, slot, at, weight = places[k]
         term = jnp.sum(tiles[k] * columns[r], axis=0, keepdims=True) * weight
         row = pl.ds(at & (table.shape[2] - 1), 1)
         table[slot, at >> shift, row, :] = table[slot, at >> shift, row, :] + term
@@ -128,18 +129,21 @@
 
 
 def first_kernel(rows_far, cols_far, count, tiles_far, times, table, times_t, columns, tiles, rows, cols, sems):
-    moves = started([(tiles_far, tiles), (rows_far, rows), (cols_far, cols)], sems)
+    parts = [pl.ds(k, TS // 4) for k in range(0, TS, TS // 4)]
+    pairs = [(rows_far, rows), (cols_far, cols)] + [(tiles_far.at[p], tiles.at[p]) for p in parts]
+    moves = started(pairs, sems)
     padded = jnp.concatenate([times[...], jnp.zeros((LANES - RB, LANES), jnp.float32)], axis=0)
     turned = padded.T
     times_t[...] = turned
     for r in range(RB):
         columns[r] = jnp.broadcast_to(turned[:, r : r + 1], (LANES, LANES))
     table[...] = jnp.zeros_like(table)
+    moves[0].wait()
     moves[1].wait()
-    moves[2].wait()
     places = placed((rows, cols, count))
-    moves[0].wait()
-    backward_terms(places, tiles, columns, table)
+    for i, move in enumerate(moves[2:]):
+        move.wait()
+        backward_terms(places, tiles, columns, table, i * TS // 4, (i + 1) * TS // 4)
 
 
 def second_kernel(rows_far, cols_far, count, tiles, cells, times_t, table, image_t, columns, rows, cols, sems):
@@ -260,7 +264,7 @@
         [shape(TABLE, *NARROW, LANES), square],
         [far, far, SM, far, VM],
         (*lists, tiles, travel_times),
-        [columns, columns, *short, pltpu.SemaphoreType.DMA((3,))],
+        [columns, columns, *short, pltpu.SemaphoreType.DMA((6,))],
         54528,
     )
     (cells,) = exchange(table)

time: 151 us -> 151 us (level)
  no operation moved by 1% of the time
where the time goes in v7:
time: 151 us; the launch traced here: 150 us
  blocking collectives  143 us (95%)
  Pallas kernels  4.89 us (3%)
    all_to_all x8, blocking collectives, swap(): lax.all_to_all(array, 'all', 0, 0, tiled=True, axis_index_groups=groups)  118 us
    all_gather x2, blocking collectives, exchange(): lax.all_gather(table.reshape((NC, SLOTS) + slot), 'all', axis=0, axis_ind...  14.7 us
    all_gather x2, blocking collectives, exchange(): lax.all_gather(swap(copies, LINES), 'all', axis=0, axis_index_groups=PAIRS)  10.9 us
    pallas_call x8, Pallas kernels, call(): pl.pallas_call(kernel, out_shape=outs, in_specs=ins, out_specs=jax.tree.m...  4.89 us

profile of v7, /device:TPU:1, one launch (start us, length us, event | category | flops | bytes accessed | tf_op | source)
XLA Modules:
  0.0 150.4 jit_solution(9393193063701097276)
XLA Ops:
  1.3 0.0 copy-start.2
  1.3 0.0 copy-done.1
  1.3 0.6 copy-done.2
  2.0 0.0 copy-done.3
  2.0 1.4 shard_map.68
  3.4 12.4 %all_gather.18 = f32[2,2,24,3,4,128]{5,2,4,3,1,0:T(8,128)S(1)} all-gather(f32[1,2,24,3,4,128]{5,2,4,3,1,0:T(8,128)S(1)} %copy.9), channel_id=1, replica_groups={{0,1},{2,3},{4,5},{6,7},{8,9},{10,11},{12,13},{14,15},{16,17},{18,19},{..., dimensions={0}, use_global_device_ids=true | all-gather | bytes 884736 | tf_op jit(solution)/shard_map/all_gather | solution.py:245
  15.8 0.0 copy-start
  15.9 17.6 %all_to_all.40.parts = f32[24,3,4,128]{3,2,1,0:T(4,128)S(1)} all-to-all(f32[24,3,4,128]{3,2,1,0:T(4,128)S(1)} %copy.10), channel_id=1, replica_groups={{0,24,2,26,4,28,6,30,8,32,10,34,12,36,14,38,16,40,18,42,20,44,22,46},{1..., dimensions={0} | all-to-all | bytes 294912 | tf_op jit(solution)/shard_map/all_to_all | solution.py:76
  33.5 16.9 %all_to_all.41.parts = f32[16,3,4,128]{3,2,1,0:T(4,128)S(1)} all-to-all(f32[16,3,4,128]{3,2,1,0:T(4,128)S(1)} %shard_map.69), channel_id=1, replica_groups={{0,96,192,288,384,480,576,672,72,168,264,360,456,552,648,744},{1,97,193..., dimensions={0} | all-to-all | bytes 196608 | tf_op jit(solution)/shard_map/all_to_all | solution.py:76
  50.4 15.7 %all_to_all.42 = f32[24,3,4,128]{3,2,1,0:T(4,128)S(1)} all-to-all(f32[24,3,4,128]{3,2,1,0:T(4,128)S(1)} %shard_map.70), channel_id=1, replica_groups={{0,24,2,26,4,28,6,30,8,32,10,34,12,36,14,38,16,40,18,42,20,44,22,46},{1..., dimensions={0} | all-to-all | bytes 294912 | tf_op jit(solution)/shard_map/all_to_all | solution.py:76
  66.1 5.4 %all-gather.cells = f32[48,3,4,128]{3,2,1,0:T(4,128)S(1)} all-gather(f32[24,3,4,128]{3,2,1,0:T(4,128)S(1)} %all_to_all.42), channel_id=2, replica_groups={{0,1},{2,3},{4,5},{6,7},{8,9},{10,11},{12,13},{14,15},{16,17},{18,19},{..., dimensions={0}, use_global_device_ids=true | all-gather | bytes 442368 | tf_op jit(solution)/shard_map/all_gather | solution.py:250
  71.5 1.2 shard_map.71
  72.8 2.3 %all_gather.21 = f32[2,2,24,7,2,128]{5,2,4,3,1,0:T(8,128)S(1)} all-gather(f32[1,2,24,7,2,128]{5,2,4,3,1,0:T(8,128)S(1)} %copy.11), channel_id=1, replica_groups={{0,1},{2,3},{4,5},{6,7},{8,9},{10,11},{12,13},{14,15},{16,17},{18,19},{..., dimensions={0}, use_global_device_ids=true | all-gather | bytes 1032192 | tf_op jit(solution)/shard_map/all_gather | solution.py:245
  75.1 0.1 copy.12
  75.2 15.3 %all_to_all.43.parts = f32[24,7,2,128]{3,2,1,0:T(2,128)S(1)} all-to-all(f32[24,7,2,128]{3,2,1,0:T(2,128)S(1)} %copy.12), channel_id=1, replica_groups={{0,24,2,26,4,28,6,30,8,32,10,34,12,36,14,38,16,40,18,42,20,44,22,46},{1..., dimensions={0} | all-to-all | bytes 344064 | tf_op jit(solution)/shard_map/all_to_all | solution.py:76
  90.5 0.1 shard_map.72
  90.6 11.2 %all_to_all.44.parts = f32[16,7,2,128]{3,2,1,0:T(2,128)S(1)} all-to-all(f32[16,7,2,128]{3,2,1,0:T(2,128)S(1)} %shard_map.72), channel_id=1, replica_groups={{0,96,192,288,384,480,576,672,72,168,264,360,456,552,648,744},{1,97,193..., dimensions={0} | all-to-all | bytes 229376 | tf_op jit(solution)/shard_map/all_to_all | solution.py:76
  101.7 0.1 shard_map.73
  101.8 15.7 %all_to_all.45 = f32[24,3,4,128]{3,2,1,0:T(4,128)S(1)} all-to-all(f32[24,3,4,128]{3,2,1,0:T(4,128)S(1)} %get-tuple-element.15), channel_id=1, replica_groups={{0,24,2,26,4,28,6,30,8,32,10,34,12,36,14,38,16,40,18,42,20,44,22,46},{1..., dimensions={0} | all-to-all | bytes 294912 | tf_op jit(solution)/shard_map/all_to_all | solution.py:76
  117.5 5.5 %all-gather.1.cells_2 = f32[48,3,4,128]{3,2,1,0:T(4,128)S(1)} all-gather(f32[24,3,4,128]{3,2,1,0:T(4,128)S(1)} %all_to_all.45), channel_id=3, replica_groups={{0,1},{2,3},{4,5},{6,7},{8,9},{10,11},{12,13},{14,15},{16,17},{18,19},{..., dimensions={0}, use_global_device_ids=true | all-gather | bytes 442368 | tf_op jit(solution)/shard_map/all_gather | solution.py:250
  123.0 1.2 shard_map.74
  124.2 13.7 %all_to_all.46 = f32[24,1,128]{2,1,0:T(1,128)S(1)} all-to-all(f32[24,1,128]{2,1,0:T(1,128)S(1)} %get-tuple-element.18), channel_id=1, replica_groups={{0,1,2,3,4,5,6,7,8,9,10,11,12,13,14,15,16,17,18,19,20,21,22,23},{24,25,..., dimensions={0} | all-to-all | bytes 24576 | tf_op jit(solution)/shard_map/all_to_all | solution.py:76
  138.0 11.5 %all_to_all.47.rows = f32[32,1,128]{2,1,0:T(1,128)S(1)} all-to-all(f32[32,1,128]{2,1,0:T(1,128)S(1)} %broadcast_in_dim.2), channel_id=1, replica_groups={{0,24,48,72,96,120,144,168,192,216,240,264,288,312,336,360,384,408,432,..., dimensions={0} | all-to-all | bytes 32768 | tf_op jit(solution)/shard_map/all_to_all | solution.py:76
  149.5 0.9 shard_map.75
  (12 shorter events, 0.3 us)
Async XLA Ops:
  0.6 0.7 copy-start.1
  1.3 0.7 copy-start.2
  1.3 0.7 copy-start.3
  15.8 55.7 %copy-start = (f32[1,16,128,128]{3,2,1,0:T(8,128)S(1)}, f32[1,16,128,128]{3,2,1,0:T(8,128)}, u32[]{:S(2)}) copy-start(f32[1,16,128,128]{3,2,1,0:T(8,128)} %param.5) | copy-start | bytes 3145732

commit v8 on v7

--- a/solution.py
+++ b/solution.py
@@ -278,12 +278,12 @@
     cells_2, sums = exchange(table)
     copies, held = call(
         third_kernel,
-        [shape(NZ * NC, 1, LANES), shape(6, 2, LANES)],
+        [shape(NY * NX, 1, LANES), shape(6, 2, LANES)],
         [SM] * 3 + [VM] * 6,
         (*lists, tiles, cells, cells_2, times_t, image_t, sums),
     )
-    rows = swap(copies, CHIPS_Z).sum(0)
-    rows = swap(jnp.broadcast_to(rows[None], (NY * NX, 1, LANES)), ALL_YX)
+    rows = swap(copies, ALL_YX).sum(0)
+    rows = swap(jnp.broadcast_to(rows[None], (NZ * NC, 1, LANES)), CHIPS_Z)
     update, ratio = call(last_kernel, [shape(2, LANES), shape(1, 1)], [VM] * 2, (rows, held))
     return update, ratio.reshape(1)
 

time: 151 us -> 152 us (level)
  blocking collectives: 143 us -> 145 us
where the time goes in v8:
time: 152 us
  blocking collectives  145 us (95%)
  Pallas kernels  4.89 us (3%)
    all_to_all x8, blocking collectives, swap(): lax.all_to_all(array, 'all', 0, 0, tiled=True, axis_index_groups=groups)  119 us
    all_gather x2, blocking collectives, exchange(): lax.all_gather(table.reshape((NC, SLOTS) + slot), 'all', axis=0, axis_ind...  14.7 us
    all_gather x2, blocking collectives, exchange(): lax.all_gather(swap(copies, LINES), 'all', axis=0, axis_index_groups=PAIRS)  10.9 us
    pallas_call x8, Pallas kernels, call(): pl.pallas_call(kernel, out_shape=outs, in_specs=ins, out_specs=jax.tree.m...  4.89 us

profile of v8, /device:TPU:1, one launch (start us, length us, event | category | flops | bytes accessed | tf_op | source)
XLA Modules:
  0.0 151.8 jit_solution(15827293512842133517)
XLA Ops:
  1.3 0.0 copy-done.1
  1.3 0.6 copy-done.2
  2.0 0.0 copy-done.3
  2.0 1.4 shard_map.68
  3.4 12.4 %all_gather.18 = f32[2,2,24,3,4,128]{5,2,4,3,1,0:T(8,128)S(1)} all-gather(f32[1,2,24,3,4,128]{5,2,4,3,1,0:T(8,128)S(1)} %copy.9), channel_id=1, replica_groups={{0,1},{2,3},{4,5},{6,7},{8,9},{10,11},{12,13},{14,15},{16,17},{18,19},{..., dimensions={0}, use_global_device_ids=true | all-gather | bytes 884736 | tf_op jit(solution)/shard_map/all_gather | solution.py:245
  15.8 0.0 copy-start
  15.9 17.6 %all_to_all.40.parts = f32[24,3,4,128]{3,2,1,0:T(4,128)S(1)} all-to-all(f32[24,3,4,128]{3,2,1,0:T(4,128)S(1)} %copy.10), channel_id=1, replica_groups={{0,24,2,26,4,28,6,30,8,32,10,34,12,36,14,38,16,40,18,42,20,44,22,46},{1..., dimensions={0} | all-to-all | bytes 294912 | tf_op jit(solution)/shard_map/all_to_all | solution.py:76
  33.5 16.9 %all_to_all.41.parts = f32[16,3,4,128]{3,2,1,0:T(4,128)S(1)} all-to-all(f32[16,3,4,128]{3,2,1,0:T(4,128)S(1)} %shard_map.69), channel_id=1, replica_groups={{0,96,192,288,384,480,576,672,72,168,264,360,456,552,648,744},{1,97,193..., dimensions={0} | all-to-all | bytes 196608 | tf_op jit(solution)/shard_map/all_to_all | solution.py:76
  50.4 15.7 %all_to_all.42 = f32[24,3,4,128]{3,2,1,0:T(4,128)S(1)} all-to-all(f32[24,3,4,128]{3,2,1,0:T(4,128)S(1)} %shard_map.70), channel_id=1, replica_groups={{0,24,2,26,4,28,6,30,8,32,10,34,12,36,14,38,16,40,18,42,20,44,22,46},{1..., dimensions={0} | all-to-all | bytes 294912 | tf_op jit(solution)/shard_map/all_to_all | solution.py:76
  66.1 5.4 %all-gather.cells = f32[48,3,4,128]{3,2,1,0:T(4,128)S(1)} all-gather(f32[24,3,4,128]{3,2,1,0:T(4,128)S(1)} %all_to_all.42), channel_id=2, replica_groups={{0,1},{2,3},{4,5},{6,7},{8,9},{10,11},{12,13},{14,15},{16,17},{18,19},{..., dimensions={0}, use_global_device_ids=true | all-gather | bytes 442368 | tf_op jit(solution)/shard_map/all_gather | solution.py:250
  71.5 1.2 shard_map.71
  72.8 2.3 %all_gather.21 = f32[2,2,24,7,2,128]{5,2,4,3,1,0:T(8,128)S(1)} all-gather(f32[1,2,24,7,2,128]{5,2,4,3,1,0:T(8,128)S(1)} %copy.11), channel_id=1, replica_groups={{0,1},{2,3},{4,5},{6,7},{8,9},{10,11},{12,13},{14,15},{16,17},{18,19},{..., dimensions={0}, use_global_device_ids=true | all-gather | bytes 1032192 | tf_op jit(solution)/shard_map/all_gather | solution.py:245
  75.1 0.1 copy.12
  75.2 15.3 %all_to_all.43.parts = f32[24,7,2,128]{3,2,1,0:T(2,128)S(1)} all-to-all(f32[24,7,2,128]{3,2,1,0:T(2,128)S(1)} %copy.12), channel_id=1, replica_groups={{0,24,2,26,4,28,6,30,8,32,10,34,12,36,14,38,16,40,18,42,20,44,22,46},{1..., dimensions={0} | all-to-all | bytes 344064 | tf_op jit(solution)/shard_map/all_to_all | solution.py:76
  90.5 0.1 shard_map.72
  90.6 11.2 %all_to_all.44.parts = f32[16,7,2,128]{3,2,1,0:T(2,128)S(1)} all-to-all(f32[16,7,2,128]{3,2,1,0:T(2,128)S(1)} %shard_map.72), channel_id=1, replica_groups={{0,96,192,288,384,480,576,672,72,168,264,360,456,552,648,744},{1,97,193..., dimensions={0} | all-to-all | bytes 229376 | tf_op jit(solution)/shard_map/all_to_all | solution.py:76
  101.7 0.1 shard_map.73
  101.8 15.7 %all_to_all.45 = f32[24,3,4,128]{3,2,1,0:T(4,128)S(1)} all-to-all(f32[24,3,4,128]{3,2,1,0:T(4,128)S(1)} %get-tuple-element.15), channel_id=1, replica_groups={{0,24,2,26,4,28,6,30,8,32,10,34,12,36,14,38,16,40,18,42,20,44,22,46},{1..., dimensions={0} | all-to-all | bytes 294912 | tf_op jit(solution)/shard_map/all_to_all | solution.py:76
  117.5 5.5 %all-gather.1.cells_2 = f32[48,3,4,128]{3,2,1,0:T(4,128)S(1)} all-gather(f32[24,3,4,128]{3,2,1,0:T(4,128)S(1)} %all_to_all.45), channel_id=3, replica_groups={{0,1},{2,3},{4,5},{6,7},{8,9},{10,11},{12,13},{14,15},{16,17},{18,19},{..., dimensions={0}, use_global_device_ids=true | all-gather | bytes 442368 | tf_op jit(solution)/shard_map/all_gather | solution.py:250
  123.0 1.2 shard_map.74
  124.2 12.4 %all_to_all.46 = f32[32,1,128]{2,1,0:T(1,128)S(1)} all-to-all(f32[32,1,128]{2,1,0:T(1,128)S(1)} %get-tuple-element.18), channel_id=1, replica_groups={{0,24,48,72,96,120,144,168,192,216,240,264,288,312,336,360,384,408,432,..., dimensions={0} | all-to-all | bytes 32768 | tf_op jit(solution)/shard_map/all_to_all | solution.py:76
  136.6 0.1 reduce_sum.29
  136.7 14.3 %all_to_all.47.rows = f32[24,1,128]{2,1,0:T(1,128)S(1)} all-to-all(f32[24,1,128]{2,1,0:T(1,128)S(1)} %broadcast_in_dim.2), channel_id=1, replica_groups={{0,1,2,3,4,5,6,7,8,9,10,11,12,13,14,15,16,17,18,19,20,21,22,23},{24,25,..., dimensions={0} | all-to-all | bytes 24576 | tf_op jit(solution)/shard_map/all_to_all | solution.py:76
  150.9 0.9 shard_map.75
  (12 shorter events, 0.2 us)
Async XLA Ops:
  0.6 0.7 copy-start.1
  1.3 0.7 copy-start.2
  1.3 0.7 copy-start.3
  15.8 55.7 %copy-start = (f32[1,16,128,128]{3,2,1,0:T(8,128)S(1)}, f32[1,16,128,128]{3,2,1,0:T(8,128)}, u32[]{:S(2)}) copy-start(f32[1,16,128,128]{3,2,1,0:T(8,128)} %param.5) | copy-start | bytes 3145732
